TPU v7x, 32 devices: a whole 2x2x4 slice. The times are simulated.
32 devices in a mesh: dp: 8 (over z, x), head: 4 (over y, core).
Axes of the slice: x: 2, y: 2, z: 4, core: 2. Of those that a mesh axis runs over, the one named last changes fastest.
Arguments:
- hidden_in: bfloat16 [8192, 768], P(('dp', 'head')), may hold values from -6 to 6
- out_cotangent: bfloat16 [8192, 768], P(('dp', 'head')), may hold values from -6 to 6
- labels: int32 [64], P(('dp', 'head')), may hold values from 0 to 2
- qkv_weight: bfloat16 [2, 3, 768, 768], P(None, None, None, 'head'), may hold values from -6 to 6
- qkv_bias: bfloat16 [2, 2, 768], P(None, None, 'head'), may hold values from -6 to 6
- out_weight: bfloat16 [2, 768, 768], P(None, 'head'), may hold values from -6 to 6
- out_bias: bfloat16 [2, 768], P(None, 'head'), may hold values from -6 to 6
- norm_gain: bfloat16 [2, 2, 768], P(None, None, 'head'), may hold values from 0.099609375 to 1.8984375
- norm_shift: bfloat16 [2, 2, 768], P(None, None, 'head'), may hold values from -6 to 6
- ffn_in: bfloat16 [2, 768, 3072], P(None, 'head'), may hold values from -6 to 6
- ffn_in_bias: bfloat16 [2, 3072], P(None, 'head'), may hold values from -6 to 6
- ffn_out: bfloat16 [2, 3072, 768], P(None, 'head'), may hold values from -6 to 6
- ffn_out_bias: bfloat16 [2, 768], P(None, 'head'), may hold values from -6 to 6
- pool_weight: bfloat16 [2, 768, 768], P(None, 'head'), may hold values from -6 to 6
- pool_bias: bfloat16 [2, 768], P(None, 'head'), may hold values from -6 to 6
- class_weight: bfloat16 [2, 768, 3], P(None, 'head'), may hold values from -6 to 6
- class_bias: bfloat16 [2, 3], replicated, may hold values from -6 to 6
Outputs:
- block_outputs: bfloat16 [2, 8192, 768], P(None, ('dp', 'head'))
- ramp_logits: float32 [2, 64, 3], P(None, ('dp', 'head'))
- input_grad: bfloat16 [8192, 768], P(('dp', 'head'))
- qkv_weight_grad: float32 [2, 3, 768, 768], P(None, None, None, 'head')
- qkv_bias_grad: float32 [2, 2, 768], P(None, None, 'head')
- out_weight_grad: float32 [2, 768, 768], P(None, 'head')
- out_bias_grad: float32 [2, 768], P(None, 'head')
- norm_gain_grad: float32 [2, 2, 768], P(None, None, 'head')
- norm_shift_grad: float32 [2, 2, 768], P(None, None, 'head')
- ffn_in_grad: float32 [2, 768, 3072], P(None, 'head')
- ffn_in_bias_grad: float32 [2, 3072], P(None, 'head')
- ffn_out_grad: float32 [2, 3072, 768], P(None, 'head')
- ffn_out_bias_grad: float32 [2, 768], P(None, 'head')
- pool_weight_grad: float32 [2, 768, 768], P(None, 'head')
- pool_bias_grad: float32 [2, 768], P(None, 'head')
- class_weight_grad: float32 [2, 768, 3], P(None, 'head')
- class_bias_grad: float32 [2, 3], replicated
All inputs are finite; a program needn't handle non-finite values.
Results may differ from a plain program's by a relative error of at most 0.015.
Values may be sent and summed in bfloat16 or wider, within the bound.
No kernel may reach another device: no remote copies, remote signals or barrier semaphores. Data moves between devices by JAX's collectives and lax.ppermute only.
A program may use at most 256 MiB of HBM per device.

v0:
```python
import jax
import jax.numpy as jnp
from jax import lax
from jax.sharding import PartitionSpec as P

D = 768
HEAD_DIM = 64
SEQ = 128
LAYERS = 2


EPS = 1e-12
ROOT_HALF = 0.7071067811865476
DENSITY_SCALE = 0.3989422804014327


def norm_forward(resid, gain_row, shift_row):
    average = jnp.mean(resid, -1, keepdims=True)
    centred = resid - average
    rstd = lax.rsqrt(jnp.mean(centred * centred, -1, keepdims=True) + EPS)
    normed = centred * rstd
    return (normed * gain_row.astype(jnp.float32) + shift_row.astype(jnp.float32), normed, rstd)


def norm_backward(incoming, normed, rstd, gain_row):
    gain_grad = jnp.sum(incoming * normed, 0)
    shift_grad = jnp.sum(incoming, 0)
    scaled = incoming * gain_row.astype(jnp.float32)
    back = rstd * (
        scaled
        - jnp.mean(scaled, -1, keepdims=True)
        - normed * jnp.mean(scaled * normed, -1, keepdims=True)
    )
    return (back, gain_grad, shift_grad)


def gelu_slope(values):
    cumulative = 0.5 * (1.0 + lax.erf(values * ROOT_HALF))
    density = jnp.exp(-0.5 * values * values) * DENSITY_SCALE
    return cumulative + values * density


def attend(queries, key_rows, values, score_scale):
    scores = (
        jnp.einsum("bqhe,bkhe->bhqk", queries, key_rows, preferred_element_type=jnp.float32)
        * score_scale
    )
    row_max = jnp.max(scores, -1, keepdims=True)
    log_total = row_max + jnp.log(jnp.sum(jnp.exp(scores - row_max), -1, keepdims=True))
    probs_low = jnp.exp(scores - log_total).astype(jnp.bfloat16)
    context = jnp.einsum("bhqk,bkhe->bqhe", probs_low, values, preferred_element_type=jnp.float32)
    return (context, log_total)


def attend_back(queries, key_rows, values, log_total, context_grad, score_scale):
    scores = (
        jnp.einsum("bqhe,bkhe->bhqk", queries, key_rows, preferred_element_type=jnp.float32)
        * score_scale
    )
    probs = jnp.exp(scores - log_total)
    probs_low = probs.astype(jnp.bfloat16)
    value_grad = jnp.einsum(
        "bhqk,bqhe->bkhe", probs_low, context_grad, preferred_element_type=jnp.float32
    )
    prob_grad = jnp.einsum(
        "bqhe,bkhe->bhqk", context_grad, values, preferred_element_type=jnp.float32
    )
    score_grad = (probs * (prob_grad - jnp.sum(prob_grad * probs, -1, keepdims=True))).astype(
        jnp.bfloat16
    )
    query_grad = (
        jnp.einsum("bhqk,bkhe->bqhe", score_grad, key_rows, preferred_element_type=jnp.float32)
        * score_scale
    )
    key_grad = (
        jnp.einsum("bhqk,bqhe->bkhe", score_grad, queries, preferred_element_type=jnp.float32)
        * score_scale
    )
    return (query_grad, key_grad, value_grad)


def project_qkv(rows, qkv_w, qkv_b):
    projected = jnp.einsum("td,sde->ste", rows, qkv_w, preferred_element_type=jnp.float32)
    bias_rows = jnp.stack([qkv_b[0], jnp.zeros_like(qkv_b[0]), qkv_b[1]]).astype(jnp.float32)
    return (projected + bias_rows[:, None, :]).astype(jnp.bfloat16)


def qkv_weight_terms(rows, qkv_rows, qkv_w):
    w_grad = jnp.einsum("td,ste->sde", rows, qkv_rows, preferred_element_type=jnp.float32)
    b_grad = jnp.stack(
        [jnp.sum(qkv_rows[0].astype(jnp.float32), 0), jnp.sum(qkv_rows[2].astype(jnp.float32), 0)]
    )
    partial_rows = jnp.einsum("ste,sde->td", qkv_rows, qkv_w, preferred_element_type=jnp.float32)
    return (w_grad, b_grad, partial_rows)


def forward_layer(layer_input, params, class_row, seq_count, score_scale):
    (
        qkv_w,
        qkv_b,
        out_w,
        out_b,
        gains,
        shifts,
        in_w,
        in_b,
        down_w,
        down_b,
        pool_w,
        pool_b,
        class_w,
    ) = params
    qkv_heads = lax.all_to_all(
        project_qkv(layer_input, qkv_w, qkv_b), "head", split_axis=2, concat_axis=1, tiled=True
    )
    group_seqs = qkv_heads.shape[1] // SEQ
    local_heads = qkv_heads.shape[2] // HEAD_DIM
    split_qkv = qkv_heads.reshape(3, group_seqs, SEQ, local_heads, HEAD_DIM)
    context, log_total = attend(split_qkv[0], split_qkv[1], split_qkv[2], score_scale)
    context_low = context.reshape(group_seqs * SEQ, local_heads * HEAD_DIM).astype(jnp.bfloat16)
    context_rows = lax.all_to_all(context_low, "head", split_axis=0, concat_axis=1, tiled=True)
    hidden = layer_input.astype(jnp.float32)
    attn_out = jnp.dot(context_rows, out_w, preferred_element_type=jnp.float32) + out_b.astype(
        jnp.float32
    )
    middle, normed_one, rstd_one = norm_forward(hidden + attn_out, gains[0], shifts[0])
    middle_low = middle.astype(jnp.bfloat16)
    pre_act = jnp.dot(middle_low, in_w, preferred_element_type=jnp.float32) + in_b.astype(
        jnp.float32
    )
    act_low = jax.nn.gelu(pre_act, approximate=False).astype(jnp.bfloat16)
    ffn_res = jnp.dot(act_low, down_w, preferred_element_type=jnp.float32) + down_b.astype(
        jnp.float32
    )
    final, normed_two, rstd_two = norm_forward(middle + ffn_res, gains[1], shifts[1])
    output = final.astype(jnp.bfloat16)
    first_rows = output.reshape(seq_count, SEQ, output.shape[1])[:, 0]
    pooled = jnp.tanh(
        jnp.dot(first_rows, pool_w, preferred_element_type=jnp.float32) + pool_b.astype(jnp.float32)
    )
    pooled_low = pooled.astype(jnp.bfloat16)
    logits = jnp.dot(pooled_low, class_w, preferred_element_type=jnp.float32) + class_row
    return dict(
        group_input=layer_input,
        split_qkv=split_qkv,
        log_total=log_total,
        context_rows=context_rows,
        normed_one=normed_one,
        rstd_one=rstd_one,
        middle_low=middle_low,
        pre_act=pre_act,
        act_low=act_low,
        normed_two=normed_two,
        rstd_two=rstd_two,
        output=output,
        first_rows=first_rows,
        pooled=pooled,
        pooled_low=pooled_low,
        logits=logits,
    )


def backward_layer(record, params, out_rows, labels, seq_count, score_scale):
    (
        qkv_w,
        qkv_b,
        out_w,
        out_b,
        gains,
        shifts,
        in_w,
        in_b,
        down_w,
        down_b,
        pool_w,
        pool_b,
        class_w,
    ) = params
    tokens = out_rows.shape[0]
    logits = record["logits"]
    classes = lax.broadcasted_iota(jnp.int32, logits.shape, 1)
    onehot = (classes == labels[:, None]).astype(jnp.float32)
    soft_probs = jax.nn.softmax(logits, axis=-1)
    logit_grad = (soft_probs - onehot).astype(jnp.bfloat16)
    class_w_grad = jnp.einsum(
        "nd,nc->dc", record["pooled_low"], logit_grad, preferred_element_type=jnp.float32
    )
    class_b_grad = jnp.sum(logit_grad.astype(jnp.float32), 0)
    pooled = record["pooled"]
    pooled_back = jnp.einsum("nc,dc->nd", logit_grad, class_w, preferred_element_type=jnp.float32)
    pool_grad = (pooled_back * (1.0 - pooled * pooled)).astype(jnp.bfloat16)
    pool_w_grad = jnp.einsum(
        "nd,ne->de", record["first_rows"], pool_grad, preferred_element_type=jnp.float32
    )
    pool_b_grad = jnp.sum(pool_grad.astype(jnp.float32), 0)
    first_grad = jnp.einsum("ne,de->nd", pool_grad, pool_w, preferred_element_type=jnp.float32)
    out_rows = out_rows.reshape(seq_count, SEQ, D).at[:, 0].add(first_grad).reshape(tokens, D)
    res_two_grad, gain_two_grad, shift_two_grad = norm_backward(
        out_rows, record["normed_two"], record["rstd_two"], gains[1]
    )
    ffn_grad = res_two_grad.astype(jnp.bfloat16)
    down_w_grad = jnp.einsum(
        "tf,td->fd", record["act_low"], ffn_grad, preferred_element_type=jnp.float32
    )
    down_b_grad = jnp.sum(ffn_grad.astype(jnp.float32), 0)
    act_grad = jnp.einsum("td,fd->tf", ffn_grad, down_w, preferred_element_type=jnp.float32)
    pre_grad = (act_grad * gelu_slope(record["pre_act"])).astype(jnp.bfloat16)
    in_w_grad = jnp.einsum(
        "td,tf->df", record["middle_low"], pre_grad, preferred_element_type=jnp.float32
    )
    in_b_grad = jnp.sum(pre_grad.astype(jnp.float32), 0)
    middle_grad = res_two_grad + jnp.einsum(
        "tf,df->td", pre_grad, in_w, preferred_element_type=jnp.float32
    )
    res_one_grad, gain_one_grad, shift_one_grad = norm_backward(
        middle_grad, record["normed_one"], record["rstd_one"], gains[0]
    )
    attn_grad = res_one_grad.astype(jnp.bfloat16)
    out_w_grad = jnp.einsum(
        "td,te->de", record["context_rows"], attn_grad, preferred_element_type=jnp.float32
    )
    out_b_grad = jnp.sum(attn_grad.astype(jnp.float32), 0)
    context_grad = jnp.einsum(
        "te,de->td", attn_grad, out_w, preferred_element_type=jnp.float32
    ).astype(jnp.bfloat16)
    context_heads = lax.all_to_all(context_grad, "head", split_axis=1, concat_axis=0, tiled=True)
    split_qkv = record["split_qkv"]
    group_seqs = split_qkv.shape[1]
    local_heads = split_qkv.shape[3]
    context_heads = context_heads.reshape(group_seqs, SEQ, local_heads, HEAD_DIM)
    query_grad, key_grad, value_grad = attend_back(
        split_qkv[0], split_qkv[1], split_qkv[2], record["log_total"], context_heads, score_scale
    )
    qkv_grad = (
        jnp.stack([query_grad, key_grad, value_grad])
        .reshape(3, group_seqs * SEQ, local_heads * HEAD_DIM)
        .astype(jnp.bfloat16)
    )
    qkv_rows = lax.all_to_all(qkv_grad, "head", split_axis=1, concat_axis=2, tiled=True)
    whole_w_grad, whole_b_grad, partial_rows = qkv_weight_terms(
        record["group_input"], qkv_rows, qkv_w
    )
    qkv_w_grad, qkv_b_grad = (
        lax.psum_scatter(
            whole_w_grad.astype(jnp.bfloat16), "head", scatter_dimension=2, tiled=True
        ).astype(jnp.float32),
        lax.psum_scatter(
            whole_b_grad.astype(jnp.bfloat16), "head", scatter_dimension=1, tiled=True
        ).astype(jnp.float32),
    )
    input_rows = res_one_grad + partial_rows
    gain_grads = jnp.stack([gain_one_grad, gain_two_grad])
    shift_grads = jnp.stack([shift_one_grad, shift_two_grad])
    locals_part = (
        qkv_w_grad,
        qkv_b_grad,
        out_w_grad,
        out_b_grad,
        gain_grads,
        shift_grads,
        in_w_grad,
        in_b_grad,
        down_w_grad,
        down_b_grad,
        pool_w_grad,
        pool_b_grad,
        class_w_grad,
    )
    return (input_rows, locals_part, class_b_grad)


def on_device(
    hidden_in,
    out_cotangent,
    labels,
    qkv_weight,
    qkv_bias,
    out_weight,
    out_bias,
    norm_gain,
    norm_shift,
    ffn_in,
    ffn_in_bias,
    ffn_out,
    ffn_out_bias,
    pool_weight,
    pool_bias,
    class_weight,
    class_bias,
):
    gathered = (
        lax.all_gather(qkv_weight, "head", axis=3, tiled=True),
        lax.all_gather(qkv_bias, "head", axis=2, tiled=True),
        lax.all_gather(out_weight, "head", axis=1, tiled=True),
        lax.all_gather(out_bias, "head", axis=1, tiled=True),
        lax.all_gather(norm_gain, "head", axis=2, tiled=True),
        lax.all_gather(norm_shift, "head", axis=2, tiled=True),
        lax.all_gather(ffn_in, "head", axis=1, tiled=True),
        lax.all_gather(ffn_in_bias, "head", axis=1, tiled=True),
        lax.all_gather(ffn_out, "head", axis=1, tiled=True),
        lax.all_gather(ffn_out_bias, "head", axis=1, tiled=True),
        lax.all_gather(pool_weight, "head", axis=1, tiled=True),
        lax.all_gather(pool_bias, "head", axis=1, tiled=True),
        lax.all_gather(class_weight, "head", axis=1, tiled=True),
    )
    tokens = hidden_in.shape[0]
    seq_count = tokens // SEQ
    score_scale = HEAD_DIM ** (-0.5)
    records = []
    layer_input = hidden_in
    for layer_idx in range(LAYERS):
        params = tuple((member[layer_idx] for member in gathered))
        record = forward_layer(
            layer_input, params, class_bias[layer_idx].astype(jnp.float32), seq_count, score_scale
        )
        records.append(record)
        layer_input = record["output"]
    out_rows = out_cotangent.astype(jnp.float32)
    summed_layers = [None] * LAYERS
    bias_locals = [None] * LAYERS
    for layer_idx in reversed(range(LAYERS)):
        params = tuple((member[layer_idx] for member in gathered))
        out_rows, parts, class_b_grad = backward_layer(
            records[layer_idx], params, out_rows, labels, seq_count, score_scale
        )
        reduced = (
            lax.psum_scatter(
                parts[2].astype(jnp.bfloat16), "head", scatter_dimension=0, tiled=True
            ).astype(jnp.float32),
            lax.psum_scatter(
                parts[3].astype(jnp.bfloat16), "head", scatter_dimension=0, tiled=True
            ).astype(jnp.float32),
            lax.psum_scatter(
                parts[4].astype(jnp.bfloat16), "head", scatter_dimension=1, tiled=True
            ).astype(jnp.float32),
            lax.psum_scatter(
                parts[5].astype(jnp.bfloat16), "head", scatter_dimension=1, tiled=True
            ).astype(jnp.float32),
            lax.psum_scatter(
                parts[6].astype(jnp.bfloat16), "head", scatter_dimension=0, tiled=True
            ).astype(jnp.float32),
            lax.psum_scatter(
                parts[7].astype(jnp.bfloat16), "head", scatter_dimension=0, tiled=True
            ).astype(jnp.float32),
            lax.psum_scatter(
                parts[8].astype(jnp.bfloat16), "head", scatter_dimension=0, tiled=True
            ).astype(jnp.float32),
            lax.psum_scatter(
                parts[9].astype(jnp.bfloat16), "head", scatter_dimension=0, tiled=True
            ).astype(jnp.float32),
            lax.psum_scatter(
                parts[10].astype(jnp.bfloat16), "head", scatter_dimension=0, tiled=True
            ).astype(jnp.float32),
            lax.psum_scatter(
                parts[11].astype(jnp.bfloat16), "head", scatter_dimension=0, tiled=True
            ).astype(jnp.float32),
            lax.psum_scatter(
                parts[12].astype(jnp.bfloat16), "head", scatter_dimension=0, tiled=True
            ).astype(jnp.float32),
        )
        summed_layers[layer_idx] = lax.psum(
            (
                parts[0],
                parts[1],
                reduced[0],
                reduced[1],
                reduced[2],
                reduced[3],
                reduced[4],
                reduced[5],
                reduced[6],
                reduced[7],
                reduced[8],
                reduced[9],
                reduced[10],
            ),
            "dp",
        )
        bias_locals[layer_idx] = class_b_grad
    class_bias_grad = lax.psum(jnp.stack(bias_locals), ("dp", "head"))
    stacked = tuple(
        (
            jnp.stack([summed_layers[index_layer][member_idx] for index_layer in range(LAYERS)])
            for member_idx in range(13)
        )
    )
    block_outputs = jnp.stack([record["output"] for record in records])
    ramp_logits = jnp.stack([record["logits"] for record in records])
    input_grad = out_rows.astype(jnp.bfloat16)
    return (
        block_outputs,
        ramp_logits,
        input_grad,
        stacked[0],
        stacked[1],
        stacked[2],
        stacked[3],
        stacked[4],
        stacked[5],
        stacked[6],
        stacked[7],
        stacked[8],
        stacked[9],
        stacked[10],
        stacked[11],
        stacked[12],
        class_bias_grad,
    )


def solution(mesh):
    return jax.shard_map(
        on_device,
        mesh=mesh,
        in_specs=(
            P(("dp", "head"), None),
            P(("dp", "head"), None),
            P(("dp", "head")),
            P(None, None, None, "head"),
            P(None, None, "head"),
            P(None, "head", None),
            P(None, "head"),
            P(None, None, "head"),
            P(None, None, "head"),
            P(None, "head", None),
            P(None, "head"),
            P(None, "head", None),
            P(None, "head"),
            P(None, "head", None),
            P(None, "head"),
            P(None, "head", None),
            P(),
        ),
        out_specs=(
            P(None, ("dp", "head"), None),
            P(None, ("dp", "head"), None),
            P(("dp", "head"), None),
            P(None, None, None, "head"),
            P(None, None, "head"),
            P(None, "head", None),
            P(None, "head"),
            P(None, None, "head"),
            P(None, None, "head"),
            P(None, "head", None),
            P(None, "head"),
            P(None, "head", None),
            P(None, "head"),
            P(None, "head", None),
            P(None, "head"),
            P(None, "head", None),
            P(),
        ),
        check_vma=False,
    )
```

profile of v0, /device:TPU:0, one launch (start us, length us, event | category | flops | bytes accessed | tf_op | source)
XLA Modules:
  0.0 1482.7 jit_solution(14826022864658275468)
XLA Ops:
  10.8 7.9 all_gather.44
  18.8 9.6 fusion.85
  28.6 9.1 all_gather.43
  37.6 5.1 all-gather.1
  42.8 5.2 all_gather.46
  48.0 5.1 all-gather
  53.3 9.5 all_gather.40
  62.8 9.9 slice_reduce_fusion.7
  84.6 23.9 %all-to-all-done = bf16[3,256,768]{1,0,2:T(4,128)(2,1)S(1)} async-done(((bf16[3,256,768]{1,0,2:T(4,128)(2,1)}), bf16[3,256,768]{1,0,2:T(4,128)(2,1)S(1)}, u32[]{:S(2)}, u32[]{:S(2)}) %all-to-all-start) | async-done | bytes 1179680 | tf_op jit(solution)/shard_map/all_to_all | solution.py:113
  116.6 9.0 fusion.86
  130.9 38.1 %all-gather.13.cloned.1.call-done = bf16[2,768,3072]{2,1,0:T(8,128)(2,1)} async-done(((bf16[2,192,3072]{2,1,0:T(8,128)(2,1)}), bf16[2,768,3072]{2,1,0:T(8,128)(2,1)}) %all-gather.13.cloned.1.call-update) | async-done | bytes 9437200 | tf_op jit(solution)/shard_map/all_gather | solution.py:298
  169.0 11.5 fusion.16
  180.5 54.2 %all-gather.15.cloned.1.call-done = bf16[2,3072,768]{2,1,0:T(8,128)(2,1)} async-done(((bf16[2,768,768]{2,1,0:T(8,128)(2,1)}), bf16[2,3072,768]{2,1,0:T(8,128)(2,1)}) %all-gather.15.cloned.1.call-update) | async-done | bytes 9437200 | tf_op jit(solution)/shard_map/all_gather | solution.py:300
  234.7 4.3 fusion.158
  254.1 24.4 %all_gather.51 = bf16[2,768,3]{2,0,1:T(2,128)(2,1)S(1)} all-gather(bf16[2,192,3]{2,0,1:T(2,128)(2,1)} %copy.210), channel_id=1, replica_groups=mesh['dp'=8,'head'=4] {'head'}, dimensions={1}, use_global_device_ids=true | all-gather | bytes 11520 | tf_op jit(solution)/shard_map/all_gather | solution.py:304
  281.6 5.3 all-gather.2
  307.1 4.1 all-to-all-start.3
  321.3 11.0 fusion.19
  347.1 4.7 fusion.164
  363.3 4.3 all-to-all-start.4
  369.9 5.0 all-to-all-done.4
  394.7 4.5 all-to-all-start.5
  401.6 29.7 %all-to-all-done.5 = bf16[3,1024,192]{2,0,1:T(4,128)(2,1)} async-done(((bf16[3,1024,192]{2,0,1:T(4,128)(2,1)}), bf16[3,1024,192]{2,0,1:T(4,128)(2,1)}, u32[]{:S(2)}, u32[]{:S(2)}) %all-to-all-start.5) | async-done | bytes 1179680 | tf_op jit(solution)/shard_map/all_to_all | solution.py:239
  431.3 4.0 copy.231
  445.7 5.3 fusion.165
  457.2 4.2 convert_bitcast_fusion
  466.3 13.0 all_to_all.130
  497.3 49.2 %all_to_all.131 = bf16[3,1024,192]{2,0,1:T(4,128)(2,1)} all-to-all(bf16[3,1024,192]{2,0,1:T(4,128)(2,1)} %copy.249), channel_id=1, replica_groups=mesh['dp'=8,'head'=4] {'head'}, dimensions={1} | all-to-all | bytes 2359296 | tf_op jit(solution)/shard_map/all_to_all | solution.py:239
  546.5 4.0 copy.251
  550.6 4.2 convert_bitcast_fusion.1
  554.9 5.2 convolution_convert_fusion.2
  561.7 4.7 convolution_convert_fusion
  589.4 3.9 copy.274
  607.7 39.0 %reduce-scatter.45.cloned.1.call-done = bf16[192,3072]{1,0:T(8,128)(2,1)} async-done(((bf16[768,3072]{1,0:T(8,128)(2,1)}), bf16[192,3072]{1,0:T(8,128)(2,1)}) %reduce-scatter.45.cloned.1.call-update) | async-done | bytes 1179664 | tf_op jit(solution)/shard_map/reduce_scatter | solution.py:339
  649.6 47.6 %reduce-scatter.49.cloned.1.call-done = bf16[768,768]{1,0:T(8,128)(2,1)} async-done(((bf16[3072,768]{1,0:T(8,128)(2,1)}), bf16[768,768]{1,0:T(8,128)(2,1)}) %reduce-scatter.49.cloned.1.call-update) | async-done | bytes 1179664 | tf_op jit(solution)/shard_map/reduce_scatter | solution.py:345
  700.0 48.0 %reduce-scatter.43.cloned.1.call-done = bf16[192,3072]{1,0:T(8,128)(2,1)} async-done(((bf16[768,3072]{1,0:T(8,128)(2,1)}), bf16[192,3072]{1,0:T(8,128)(2,1)}) %reduce-scatter.43.cloned.1.call-update) | async-done | bytes 1179664 | tf_op jit(solution)/shard_map/reduce_scatter | solution.py:339
  751.0 47.5 %reduce-scatter.47.cloned.1.call-done = bf16[768,768]{1,0:T(8,128)(2,1)} async-done(((bf16[3072,768]{1,0:T(8,128)(2,1)}), bf16[768,768]{1,0:T(8,128)(2,1)}) %reduce-scatter.47.cloned.1.call-update) | async-done | bytes 1179664 | tf_op jit(solution)/shard_map/reduce_scatter | solution.py:345
  807.0 39.6 %psum.215 = f32[2,3]{1,0:T(2,128)} all-reduce(f32[2,3]{1,0:T(2,128)} %pad_maximum_fusion.23), channel_id=1, replica_groups=mesh['dp'=8,'head'=4] {'dp','head'}, use_global_device_ids=true, to_apply=%region_100.0 | all-reduce | flops 6 | bytes 48 | tf_op jit(solution)/shard_map/psum | solution.py:380
  852.5 12.3 reduce-scatter.69.cloned.1.call-done
  865.7 21.3 %reduce-scatter.67.cloned.1.call-done = bf16[192,3]{1,0:T(8,128)(2,1)} async-done(((bf16[768,3]{1,0:T(8,128)(2,1)}), bf16[192,3]{1,0:T(8,128)(2,1)}) %reduce-scatter.67.cloned.1.call-update) | async-done | bytes 1168
  887.9 10.9 all-reduce.10
  899.4 9.7 reduce-scatter.57.cloned.1.call-done
  910.0 21.4 %reduce-scatter.59.cloned.1.call-done = bf16[192,2]{1,0:T(8,128)(2,1)} async-done(((bf16[768,2]{1,0:T(8,128)(2,1)}), bf16[192,2]{1,0:T(8,128)(2,1)}) %reduce-scatter.59.cloned.1.call-update) | async-done | bytes 784
  932.2 21.3 %reduce-scatter.63.cloned.1.call-done = bf16[192,2]{1,0:T(8,128)(2,1)} async-done(((bf16[768,2]{1,0:T(8,128)(2,1)}), bf16[192,2]{1,0:T(8,128)(2,1)}) %reduce-scatter.63.cloned.1.call-update) | async-done | bytes 784
  958.4 17.4 %reduce-scatter.55.cloned.1.call-done = bf16[192,2]{1,0:T(8,128)(2,1)} async-done(((bf16[768,2]{1,0:T(8,128)(2,1)}), bf16[192,2]{1,0:T(8,128)(2,1)}) %reduce-scatter.55.cloned.1.call-update) | async-done | bytes 784
  976.7 38.7 %all-reduce.8 = (f32[1,2,192]{2,1,0:T(2,128)S(1)}, f32[1,2,192]{2,1,0:T(2,128)S(1)}, f32[1,192]{1,0:T(1,128)S(1)}, f32[1,192]{1,0:T(1,128)S(1)}, f32[1,2,192]{2,...) all-reduce(f32[1,2,192]{2,1,0:T(2,128)S(1)} %bitcast_convert_fusion, ...), channel_id=1, replica_groups=mesh['dp'=8,'head'=4] {'dp'}, use_global_device_ids=true, to_apply=%region_37.0 | all-reduce | flops 6144 | bytes 49152 | tf_op jit(solution)/shard_map/psum | solution.py:361
  1020.2 442.4 %all-reduce.13.cloned.1.call-done = (f32[1,3,768,192]{2,3,1,0:T(8,128)}, f32[1,3,768,192]{2,3,1,0:T(8,128)}, f32[1,192,768]{2,1,0:T(8,128)}, f32[1,192,768]{2,1,...) async-done(((f32[1,3,768,192]{2,3,1,0:T(8,128)}, ...) | async-done | bytes 15335440 | tf_op jit(solution)/shard_map/psum | solution.py:361
  1462.6 4.4 pad_maximum_fusion.2
  (577 shorter events, 250.4 us)
Async XLA Ops:
  7.2 66.4 %all-gather.9.cloned.1.call-start = ((), (), s32[]{:S(2)}) async-start(), calls=%async_computation.26 | async-start | bytes 8847360 | tf_op jit(solution)/shard_map/all_gather | solution.py:292
  7.9 117.7 %all-gather.11.cloned.1.call-start = ((), (), s32[]{:S(2)}) async-start(), calls=%async_computation.27 | async-start | bytes 2949120 | tf_op jit(solution)/shard_map/all_gather | solution.py:294
  8.7 160.3 %all-gather.13.cloned.1.call-start = ((), (), s32[]{:S(2)}) async-start(), calls=%async_computation.28 | async-start | bytes 11796480 | tf_op jit(solution)/shard_map/all_gather | solution.py:298
  9.4 38.5 %copy-start.117 = (bf16[2,192]{1,0:T(2,128)(2,1)S(1)}, bf16[2,192]{1,0:T(2,128)(2,1)}, u32[]{:S(2)}) copy-start(bf16[2,192]{1,0:T(2,128)(2,1)} %param.27) | copy-start | bytes 2308
  9.5 43.7 %copy-start.110 = (bf16[2,2,192]{2,1,0:T(2,128)(2,1)S(1)}, bf16[2,2,192]{2,1,0:T(2,128)(2,1)}, u32[]{:S(2)}) copy-start(bf16[2,2,192]{2,1,0:T(2,128)(2,1)} %param.25) | copy-start | bytes 4612
  9.5 225.2 %all-gather.15.cloned.1.call-start = ((), (), s32[]{:S(2)}) async-start(), calls=%async_computation.29 | async-start | bytes 11796480 | tf_op jit(solution)/shard_map/all_gather | solution.py:300
  10.0 63.5 %copy-start.46 = (bf16[256,768]{1,0:T(8,128)(2,1)S(1)}, bf16[256,768]{1,0:T(8,128)(2,1)}, u32[]{:S(2)}) copy-start(bf16[256,768]{1,0:T(8,128)(2,1)} %param.21) | copy-start | bytes 1179652
  10.1 301.4 %all-gather.17.cloned.1.call-start = ((), (), s32[]{:S(2)}) async-start(), calls=%async_computation.30 | async-start | bytes 2949120 | tf_op jit(solution)/shard_map/all_gather | solution.py:302
  79.0 29.5 %all-to-all-start = ((bf16[3,256,768]{1,0,2:T(4,128)(2,1)}), bf16[3,256,768]{1,0,2:T(4,128)(2,1)S(1)}, u32[]{:S(2)}, u32[]{:S(2)}) async-start(bf16[3,256,768]{1,0,2:T(4,128)(2,1)} %copy.184), calls=%async_computation | async-start | bytes 3145728 | tf_op jit(solution)/shard_map/all_to_all | solution.py:113
  113.0 56.0 %copy-start.58 = (f32[768]{0:T(1024)S(1)}, f32[768]{0:T(1024)}, u32[]{:S(2)}) copy-start(f32[768]{0:T(1024)} %get-tuple-element.136) | copy-start | bytes 9220
  113.0 56.0 %copy-start.88 = (f32[1,3072]{1,0:T(1,128)S(1)}, f32[1,3072]{1,0:T(1,128)}, u32[]{:S(2)}) copy-start(f32[1,3072]{1,0:T(1,128)} %get-tuple-element.201) | copy-start | bytes 36868
  113.0 15.5 %all-to-all-start.1 = ((bf16[4,256,192]{1,2,0:T(8,128)(2,1)}), bf16[4,256,192]{1,2,0:T(8,128)(2,1)S(1)}, u32[]{:S(2)}, u32[]{:S(2)}) async-start(bf16[4,256,192]{1,2,0:T(8,128)(2,1)} %copy.191), calls=%async_computation.1 | async-start | bytes 786432 | tf_op jit(solution)/shard_map/all_to_all | solution.py:121
  125.6 109.1 %copy-start.52 = (f32[768]{0:T(1024)}, f32[768]{0:T(1024)S(1)}, u32[]{:S(2)}) copy-start(f32[768]{0:T(1024)S(1)} %get-tuple-element.132) | copy-start | bytes 9220
  125.6 113.7 %copy-start.50 = (f32[768]{0:T(1024)}, f32[768]{0:T(1024)S(1)}, u32[]{:S(2)}) copy-start(f32[768]{0:T(1024)S(1)} %get-tuple-element.131) | copy-start | bytes 9220
  128.5 52.0 %copy-start.33 = (bf16[4,256,192]{1,2,0:T(8,128)(2,1)}, bf16[4,256,192]{1,2,0:T(8,128)(2,1)S(1)}, u32[]{:S(2)}) copy-start(bf16[4,256,192]{1,2,0:T(8,128)(2,1)S(1)} %all-to-all-done.1) | copy-start | bytes 1179652
  130.6 104.1 %copy-start.6 = (f32[256,768]{1,0:T(8,128)}, f32[256,768]{1,0:T(8,128)S(1)}, u32[]{:S(2)}) copy-start(f32[256,768]{1,0:T(8,128)S(1)} %get-tuple-element.212) | copy-start | bytes 2359300
  130.6 104.0 %copy-start.70 = (f32[256]{0:T(256)}, f32[256]{0:T(256)S(1)}, u32[]{:S(2)}) copy-start(f32[256]{0:T(256)S(1)} %broadcast_multiply_fusion.9) | copy-start | bytes 3076
  130.9 103.8 %copy-start.80 = (f32[256]{0:T(256)}, f32[256]{0:T(256)S(1)}, u32[]{:S(2)}) copy-start(f32[256]{0:T(256)S(1)} %add_rsqrt_fusion.3) | copy-start | bytes 3076
  169.0 65.7 %copy-start.106 = (f32[768]{0:T(1024)S(1)}, f32[768]{0:T(1024)}, u32[]{:S(2)}) copy-start(f32[768]{0:T(1024)} %get-tuple-element.144) | copy-start | bytes 9220
  245.7 48.9 %all-to-all-start.2 = ((bf16[3,256,768]{1,0,2:T(4,128)(2,1)}), bf16[3,256,768]{1,0,2:T(4,128)(2,1)S(1)}, u32[]{:S(2)}, u32[]{:S(2)}) async-start(bf16[3,256,768]{1,0,2:T(4,128)(2,1)} %copy.197), calls=%async_computation.2 | async-start | bytes 3145728 | tf_op jit(solution)/shard_map/all_to_all | solution.py:113
  307.1 11.6 all-to-all-start.3
  311.2 284.0 %reduce-scatter.41.cloned.1.call-start = ((), (), s32[]{:S(2)}) async-start(), calls=%async_computation.34 | async-start | bytes 1474560 | tf_op jit(solution)/shard_map/reduce_scatter | solution.py:327
  363.3 11.6 all-to-all-start.4
  367.6 229.5 %reduce-scatter.53.cloned.1.call-start = ((), (), s32[]{:S(2)}) async-start(), calls=%async_computation.40 | async-start | bytes 1474560 | tf_op jit(solution)/shard_map/reduce_scatter | solution.py:351
  394.7 36.5 %all-to-all-start.5 = ((bf16[3,1024,192]{2,0,1:T(4,128)(2,1)}), bf16[3,1024,192]{2,0,1:T(4,128)(2,1)}, u32[]{:S(2)}, u32[]{:S(2)}) async-start(bf16[3,1024,192]{2,0,1:T(4,128)(2,1)} %copy.229), calls=%async_computation.5 | async-start | bytes 4194304 | tf_op jit(solution)/shard_map/all_to_all | solution.py:239
  399.2 199.7 %reduce-scatter.51.cloned.1.call-start = ((), (), s32[]{:S(2)}) async-start(), calls=%async_computation.39 | async-start | bytes 1474560 | tf_op jit(solution)/shard_map/reduce_scatter | solution.py:351
  401.6 199.2 %reduce-scatter.39.cloned.1.call-start = ((), (), s32[]{:S(2)}) async-start(), calls=%async_computation.33 | async-start | bytes 1474560 | tf_op jit(solution)/shard_map/reduce_scatter | solution.py:327
  456.7 145.8 %reduce-scatter.37.cloned.1.call-start = ((), (), s32[]{:S(2)}) async-start(), calls=%async_computation.32 | async-start | bytes 4423680 | tf_op jit(solution)/shard_map/reduce_scatter | solution.py:244
  461.4 143.7 %reduce-scatter.35.cloned.1.call-start = ((), (), s32[]{:S(2)}) async-start(), calls=%async_computation.31 | async-start | bytes 4423680 | tf_op jit(solution)/shard_map/reduce_scatter | solution.py:244
  497.3 53.3 %copy-start.47 = (bf16[256,768]{1,0:T(8,128)(2,1)S(1)}, bf16[256,768]{1,0:T(8,128)(2,1)}, u32[]{:S(2)}) copy-start(bf16[256,768]{1,0:T(8,128)(2,1)} %param.21) | copy-start | bytes 1179652
  554.8 91.8 %reduce-scatter.45.cloned.1.call-start = ((), (), s32[]{:S(2)}) async-start(), calls=%async_computation.36 | async-start | bytes 5898240 | tf_op jit(solution)/shard_map/reduce_scatter | solution.py:339
  560.1 137.0 %reduce-scatter.49.cloned.1.call-start = ((), (), s32[]{:S(2)}) async-start(), calls=%async_computation.38 | async-start | bytes 5898240 | tf_op jit(solution)/shard_map/reduce_scatter | solution.py:345
  566.5 181.6 %reduce-scatter.43.cloned.1.call-start = ((), (), s32[]{:S(2)}) async-start(), calls=%async_computation.35 | async-start | bytes 5898240 | tf_op jit(solution)/shard_map/reduce_scatter | solution.py:339
  571.6 226.8 %reduce-scatter.47.cloned.1.call-start = ((), (), s32[]{:S(2)}) async-start(), calls=%async_computation.37 | async-start | bytes 5898240 | tf_op jit(solution)/shard_map/reduce_scatter | solution.py:345
  576.9 273.7 %reduce-scatter.61.cloned.1.call-start = ((), (), s32[]{:S(2)}) async-start(), calls=%async_computation.44 | async-start | bytes 245760
  578.5 273.1 %reduce-scatter.65.cloned.1.call-start = ((), (), s32[]{:S(2)}) async-start(), calls=%async_computation.46 | async-start | bytes 245760
  579.4 285.4 %reduce-scatter.69.cloned.1.call-start = ((), (), s32[]{:S(2)}) async-start(), calls=%async_computation.48 | async-start | bytes 245760
  580.5 306.5 %reduce-scatter.67.cloned.1.call-start = ((), (), s32[]{:S(2)}) async-start(), calls=%async_computation.47 | async-start | bytes 245760
  581.6 327.5 %reduce-scatter.57.cloned.1.call-start = ((), (), s32[]{:S(2)}) async-start(), calls=%async_computation.42 | async-start | bytes 245760
  587.5 343.9 %reduce-scatter.59.cloned.1.call-start = ((), (), s32[]{:S(2)}) async-start(), calls=%async_computation.43 | async-start | bytes 245760
  588.4 365.1 %reduce-scatter.63.cloned.1.call-start = ((), (), s32[]{:S(2)}) async-start(), calls=%async_computation.45 | async-start | bytes 245760
  589.4 386.4 %reduce-scatter.55.cloned.1.call-start = ((), (), s32[]{:S(2)}) async-start(), calls=%async_computation.41 | async-start | bytes 245760
  595.2 867.4 %all-reduce.13.cloned.1.call-start = ((), (), s32[]{:S(2)}) async-start(), calls=%async_computation.49 | async-start | bytes 30670848 | tf_op jit(solution)/shard_map/psum | solution.py:361
  801.3 46.5 %copy-start.3 = (f32[256,768]{1,0:T(8,128)S(1)}, f32[256,768]{1,0:T(8,128)}, u32[]{:S(2)}) copy-start(f32[256,768]{1,0:T(8,128)} %copy-done.2) | copy-start | bytes 2359300
  801.3 46.5 %copy-start.49 = (f32[768]{0:T(1024)S(1)}, f32[768]{0:T(1024)}, u32[]{:S(2)}) copy-start(f32[768]{0:T(1024)} %get-tuple-element.129) | copy-start | bytes 9220
  801.3 46.5 %copy-start.63 = (f32[768]{0:T(1024)S(1)}, f32[768]{0:T(1024)}, u32[]{:S(2)}) copy-start(f32[768]{0:T(1024)} %get-tuple-element.133) | copy-start | bytes 9220
  801.4 153.1 %copy-start.12 = (f32[256,768]{1,0:T(8,128)S(1)}, f32[256,768]{1,0:T(8,128)}, u32[]{:S(2)}) copy-start(f32[256,768]{1,0:T(8,128)} %copy-done.11) | copy-start | bytes 2359300
  801.4 153.1 %copy-start.16 = (bf16[3,256,4,192]{1,3,2,0:T(8,128)(2,1)S(1)}, bf16[3,256,4,192]{1,3,2,0:T(8,128)(2,1)}, u32[]{:S(2)}) copy-start(bf16[3,256,4,192]{1,3,2,0:T(8,128)(2,1)} %copy.251) | copy-start | bytes 3538948
  (116 other events, 569.8 us)
Sparse Core Ops, SparseCore 0:
  9.6 57.8 all-gather.8
  69.1 29.8 all-gather.10
  100.5 68.4 all-gather.12
  170.4 64.2 all-gather.14
  236.1 30.2 all-gather.16
  358.7 25.7 reduce-scatter.40
  387.2 32.1 reduce-scatter.52
  421.9 25.7 reduce-scatter.50
  456.9 27.6 reduce-scatter.38
  487.5 59.6 reduce-scatter.36
  554.9 40.6 reduce-scatter.34
  598.7 47.9 reduce-scatter.44
  649.3 47.8 reduce-scatter.48
  700.2 47.8 reduce-scatter.42
  750.6 47.8 reduce-scatter.46
  800.8 19.7 reduce-scatter.60
  822.9 19.8 reduce-scatter.64
  845.1 19.6 reduce-scatter.68
  867.2 19.7 reduce-scatter.66
  889.3 19.7 reduce-scatter.56
  911.6 19.7 reduce-scatter.58
  933.8 19.7 reduce-scatter.62
  956.0 19.7 reduce-scatter.54
  983.2 479.2 all-reduce.12
where the time goes:
time: 1490 us; the launch traced here: 1480 us
  waiting for transfers between devices  888 us (60%)
  blocking collectives  223 us (15%)
  matrix products  122 us (8%)
  local copies, waits for them, and re-layouts  112 us (8%)
  other arithmetic  94.3 us (6%)
  starting transfers between devices  25.5 us (2%)
  between operations  17.7 us (1%)
    psum x1, waiting for transfers between devices, on_device(): lax.psum((parts[0], parts[1], reduced[0], reduced[1], reduced[2], reduced...  442 us
    unnamed x32, waiting for transfers between devices  107 us
    reduce_scatter x2, waiting for transfers between devices, on_device(): lax.psum_scatter(parts[8].astype(jnp.bfloat16), 'head', scatter_dimension...  95.1 us
    reduce_scatter x2, waiting for transfers between devices, on_device(): lax.psum_scatter(parts[6].astype(jnp.bfloat16), 'head', scatter_dimension...  87 us
    all_gather x1, waiting for transfers between devices, on_device(): lax.all_gather(ffn_out, 'head', axis=1, tiled=True)  54.2 us
    all_to_all x1, blocking collectives, backward_layer(): lax.all_to_all(qkv_grad, 'head', split_axis=1, concat_axis=2, tiled=True)  49.2 us
    another operation x31, other arithmetic, on_device(): jnp.stack([summed_layers[index_layer][member_idx] for index_layer in rang...  40.1 us
    psum x1, blocking collectives, on_device(): class_bias_grad = lax.psum(jnp.stack(bias_locals), ('dp', 'head'))  39.6 us
  transfers between devices with their start and end apart: 30, of which 18 were waited for; matrix products, arithmetic and copies ran while one was open for 18% of the time, Pallas kernels for 0%

commit v1 on v0

v1 whole, which is shorter than its diff:
```python
import functools

import jax
import jax.numpy as jnp
from jax import lax
from jax.experimental import pallas as pl
from jax.experimental.pallas import tpu as pltpu
from jax.sharding import PartitionSpec as P

D = 768
FF = 3072
HEAD_DIM = 64
SEQ = 128
LAYERS = 2
SHARDS = 4
PART = D // SHARDS
POOL_PART = PART // 4
PIECES = 8
CLASSES = 3
EPS = 1e-12
ROOT_HALF = 0.7071067811865476
DENSITY_SCALE = 0.3989422804014327
F32 = jnp.float32
BF16 = jnp.bfloat16
AXES = ("dp", "head")
VMEM_LIMIT = 58 * 1024 * 1024

QB, VB, OB, G0, G1, S0, S1, FB, PB, CW = 0, 1, 2, 3, 4, 5, 6, 11, 12, 13


def dot(left, right, dims):
    return lax.dot_general(left, right, ((dims[:1], dims[1:]), ((), ())), preferred_element_type=F32)


def nn(left, right):
    return dot(left, right, (1, 0))


def nt(left, right):
    return dot(left, right, (1, 1))


def tn(left, right):
    return dot(left, right, (0, 0))


def normalise(resid):
    centred = resid - jnp.mean(resid, -1, keepdims=True)
    rstd = lax.rsqrt(jnp.mean(centred * centred, -1, keepdims=True) + EPS)
    return centred * rstd, rstd


def norm_back(incoming, normed, rstd, gain):
    scaled = incoming * gain
    back = rstd * (
        scaled
        - jnp.mean(scaled, -1, keepdims=True)
        - normed * jnp.mean(scaled * normed, -1, keepdims=True)
    )
    gain_grad = jnp.sum(incoming * normed, 0, keepdims=True)
    shift_grad = jnp.sum(incoming, 0, keepdims=True)
    return back, gain_grad, shift_grad


def cost(micros):
    return pl.CostEstimate(flops=0, bytes_accessed=int(micros * 3.5e6), transcendentals=0)


def shard_index():
    return lax.axis_index("head")


def quarter_index():
    return lax.axis_index("dp") & 3


def piece_index():
    place = lax.axis_index("dp")
    return ((place & 1) << 2) | (place & 2) | ((place >> 2) & 1)


def pack_attn_kernel(qkv_ref, out_ref, own_ref, quarter_ref):
    for part in range(3):
        own_ref[part] = qkv_ref[part].T
    own_ref[3] = out_ref[...]
    quarter_ref[...] = own_ref[quarter_index()]


def pack_attn(layer, qkv_weight, out_weight):
    return pl.pallas_call(
        pack_attn_kernel,
        grid=(1,),
        out_shape=(
            jax.ShapeDtypeStruct((4, PART, D), BF16),
            jax.ShapeDtypeStruct((PART, D), BF16),
        ),
        in_specs=[layer_block(layer, shape) for shape in ((3, D, PART), (PART, D))],
        out_specs=(
            pl.BlockSpec((4, PART, D), lambda step: (0, 0, 0)),
            pl.BlockSpec((PART, D), lambda step: (0, 0)),
        ),
        compiler_params=pltpu.CompilerParams(vmem_limit_bytes=VMEM_LIMIT),
        cost_estimate=cost(3),
        name="pack_attn%d" % layer,
    )(qkv_weight, out_weight)


FFN_ROWS = 2 * PART + POOL_PART


def pack_ffn_kernel(in_ref, down_ref, pool_ref, own_ref, quarter_ref):
    for index in range(4):
        own_ref[index, 0:PART] = in_ref[:, index * D : (index + 1) * D]
        own_ref[index, PART : 2 * PART] = down_ref[index * PART : (index + 1) * PART]
        own_ref[index, 2 * PART : FFN_ROWS] = pool_ref[
            index * POOL_PART : (index + 1) * POOL_PART
        ]
    quarter_ref[...] = own_ref[quarter_index()]


def layer_block(layer, shape):
    zeros = (0,) * len(shape)
    return pl.BlockSpec((None, *shape), lambda step: (layer, *zeros))


def pack_ffn(layer, ffn_in, ffn_out, pool_weight):
    return pl.pallas_call(
        pack_ffn_kernel,
        grid=(1,),
        out_shape=(
            jax.ShapeDtypeStruct((4, FFN_ROWS, D), BF16),
            jax.ShapeDtypeStruct((FFN_ROWS, D), BF16),
        ),
        in_specs=[layer_block(layer, shape) for shape in ((PART, FF), (D, D), (PART, D))],
        out_specs=(
            pl.BlockSpec((4, FFN_ROWS, D), lambda step: (0, 0, 0)),
            pl.BlockSpec((FFN_ROWS, D), lambda step: (0, 0)),
        ),
        compiler_params=pltpu.CompilerParams(vmem_limit_bytes=VMEM_LIMIT),
        cost_estimate=cost(3),
        name="pack_ffn%d" % layer,
    )(ffn_in, ffn_out, pool_weight)


def flip(mesh, axis, bit):
    dp, head = mesh.shape["dp"], mesh.shape["head"]
    pairs = []
    for place in range(dp):
        for shard in range(head):
            to_place = place ^ bit if axis == "dp" else place
            to_shard = shard ^ bit if axis == "head" else shard
            pairs.append((place * head + shard, to_place * head + to_shard))
    return pairs


class Moves:
    def __init__(self, mesh):
        self.mesh = mesh

    def core(self, value):
        return lax.ppermute(value, AXES, flip(self.mesh, "head", 1))

    def row(self, value):
        return lax.ppermute(value, AXES, flip(self.mesh, "head", 2))

    def place(self, value, bit):
        return lax.ppermute(value, AXES, flip(self.mesh, "dp", bit))


    def gather(self, value):
        for axis in ("head", "dp"):
            bit = 1
            while bit < self.mesh.shape[axis]:
                came = lax.ppermute(value, AXES, flip(self.mesh, axis, bit))
                value = jnp.concatenate([value, came], 0)
                bit *= 2
        return value


def gather_weights(moves, own, quarter, last_bit):
    near = moves.core(own)
    far = [None] * 4
    far[0] = moves.row(quarter)
    far[1] = moves.place(far[0], 1)
    far[2] = moves.place(far[0], 2)
    far[3] = moves.place(far[2], 1) if last_bit == 1 else moves.place(far[1], 2)
    return (own, near, *far, *[moves.core(piece) for piece in far])


def load_attn_weights(refs, slots, sems):
    here = quarter_index()
    own, near, *pieces = refs
    copies = [
        [pltpu.make_async_copy(own, slots.at[0], sems.at[0])],
        [pltpu.make_async_copy(near, slots.at[1], sems.at[1])],
        [],
        [],
    ]
    for index, piece in enumerate(pieces):
        slot, relative = 2 + index // 4, index % 4
        copies[slot].append(
            pltpu.make_async_copy(piece, slots.at[slot, here ^ relative], sems.at[2 + index])
        )
    for group in copies:
        for item in group:
            item.start()
    return copies


def attn_forward_kernel(layer, x_ref, shard_small, small, *refs):
    weights = refs[:10]
    qkv_ref, probs_ref, context_ref, context_send_ref = refs[10:14]
    normed_ref, rstd_ref, low_ref, parts_ref, parts_send_ref = refs[14:19]
    slots, all_parts, sems = refs[19:]
    copies = load_attn_weights(weights, slots, sems)
    shard = shard_index()
    x = x_ref[...]
    total = x.astype(F32) + small[layer, OB : OB + 1].astype(F32)
    for slot in range(4):
        for item in copies[slot]:
            item.wait()
        biases = shard_small[shard ^ slot, layer]
        parts = []
        for part in range(3):
            value = nt(x, slots[slot, part])
            if part != 1:
                row = QB if part == 0 else VB
                value = value + biases[row : row + 1].astype(F32)
            value = value.astype(BF16)
            qkv_ref[slot, part] = value
            parts.append(value)
        query, key, val = parts
        seq_rows = []
        for seq in range(2):
            rows = slice(seq * SEQ, (seq + 1) * SEQ)
            heads = []
            for head in range(PART // HEAD_DIM):
                cols = slice(head * HEAD_DIM, (head + 1) * HEAD_DIM)
                scores = nt(query[rows, cols], key[rows, cols]) * HEAD_DIM ** (-0.5)
                shifted = jnp.exp(scores - jnp.max(scores, -1, keepdims=True))
                probs = shifted / jnp.sum(shifted, -1, keepdims=True)
                probs_ref[slot, seq * 3 + head] = probs
                heads.append(nn(probs.astype(BF16), val[rows, cols]))
            seq_rows.append(jnp.concatenate(heads, -1))
        context = jnp.concatenate(seq_rows, 0).astype(BF16)
        target = context_send_ref if slot & 1 else context_ref
        target[slot >> 1] = context
        total = total + nn(context, slots[slot, 3])
    normed, rstd = normalise(total)
    normed_ref[...] = normed
    rstd_ref[...] = rstd
    middle = normed * small[layer, G0 : G0 + 1].astype(F32) + small[layer, S0 : S0 + 1].astype(F32)
    low = middle.astype(BF16)
    low_ref[...] = low
    for part in range(SHARDS):
        all_parts[part] = low[:, part * PART : (part + 1) * PART]
    for slot in range(4):
        target = parts_send_ref if slot & 1 else parts_ref
        target[slot >> 1] = all_parts[shard ^ slot]


def vmem():
    return pl.BlockSpec(memory_space=pltpu.VMEM)


def anywhere():
    return pl.BlockSpec(memory_space=pl.ANY)


def attn_forward(layer, x, shard_small, small, weights):
    tokens = x.shape[0]
    shapes = (
        ((4, 3, tokens, PART), BF16),
        ((4, 6, SEQ, SEQ), F32),
        ((2, tokens, PART), BF16),
        ((2, tokens, PART), BF16),
        ((tokens, D), F32),
        ((tokens, 1), F32),
        ((tokens, D), BF16),
        ((2, tokens, PART), BF16),
        ((2, tokens, PART), BF16),
    )
    return pl.pallas_call(
        functools.partial(attn_forward_kernel, layer),
        out_shape=tuple(jax.ShapeDtypeStruct(*item) for item in shapes),
        in_specs=[vmem()] * 3 + [anywhere()] * 10,
        out_specs=tuple(vmem() for _ in shapes),
        scratch_shapes=[
            pltpu.VMEM((4, 4, PART, D), BF16),
            pltpu.VMEM((SHARDS, tokens, PART), BF16),
            pltpu.SemaphoreType.DMA((10,)),
        ],
        compiler_params=pltpu.CompilerParams(vmem_limit_bytes=VMEM_LIMIT),
        cost_estimate=cost(13),
        name="attn_forward%d" % layer,
    )(x, shard_small, small, *weights)


def load_ffn_weights(refs, up, down, pool, sems):
    here = quarter_index()
    shard = shard_index()
    own, near, *pieces = refs
    copies = []

    def copy(src, dst):
        copies.append(pltpu.make_async_copy(src, dst, sems.at[len(copies)]))
        copies[-1].start()

    def rows_of(owner):
        return pl.ds(pl.multiple_of(owner * PART, PART), PART)

    for slot, whole in ((0, own), (1, near)):
        owner = shard ^ slot
        copy(whole.at[:, 0:PART], up.at[:, rows_of(owner)])
        copy(whole.at[:, PART : 2 * PART], down.at[owner])
        if pool is not None:
            copy(whole.at[:, 2 * PART : FFN_ROWS], pool.at[owner])
    for index, piece in enumerate(pieces):
        owner, block = shard ^ (2 + index // 4), here ^ (index % 4)
        copy(piece.at[0:PART], up.at[block, rows_of(owner)])
        copy(piece.at[PART : 2 * PART], down.at[owner, block])
        if pool is not None:
            copy(piece.at[2 * PART : FFN_ROWS], pool.at[owner, block])
    return copies


def ffn_forward_kernel(layer, labels_ref, class_bias_ref, normed_ref, low_ref, small, in_bias, *refs):
    weights = refs[:10]
    act_ref, act_send_ref, slope_ref, normed_two_ref, rstd_two_ref, out_ref = refs[10:16]
    logits_ref, ramp_ref, first_grad_ref = refs[16:19]
    up, down, pool, acts, sems = refs[19:]
    copies = load_ffn_weights(weights, up, down, pool, sems)
    normed = normed_ref[...]
    low = low_ref[...]

    def row(index):
        return small[layer, index : index + 1].astype(F32)

    total = normed * row(G0) + row(S0) + row(FB)
    for item in copies:
        item.wait()
    for block in range(4):
        pre_act = nn(low, up[block]) + in_bias[layer, block : block + 1].astype(F32)
        cumulative = 0.5 * (1.0 + lax.erf(pre_act * ROOT_HALF))
        act = (pre_act * cumulative).astype(BF16)
        density = jnp.exp(-0.5 * pre_act * pre_act) * DENSITY_SCALE
        acts[block] = act
        slope_ref[block] = cumulative + pre_act * density
        total = total + nn(act, down[block].reshape(D, D))
    shard = shard_index()
    for slot in range(4):
        target = act_send_ref if slot & 1 else act_ref
        target[slot >> 1] = acts[shard ^ slot]
    normed_two, rstd_two = normalise(total)
    normed_two_ref[...] = normed_two
    rstd_two_ref[...] = rstd_two
    output = (normed_two * row(G1) + row(S1)).astype(BF16)
    out_ref[...] = output

    first = jnp.concatenate([output[0:1], output[SEQ : SEQ + 1]], 0).astype(F32)
    first = jnp.concatenate([first, jnp.zeros((14, D), F32)], 0).astype(BF16)
    pool_weight = pool[...].reshape(D, D)
    pooled = jnp.tanh(nn(first, pool_weight) + row(PB))
    pooled_low = pooled.astype(BF16)
    wide = pooled_low.astype(F32)
    lanes = lax.broadcasted_iota(jnp.int32, (16, 128), 1)
    rows = lax.broadcasted_iota(jnp.int32, (16, 128), 0)
    logits = jnp.zeros((16, 128), F32)
    for cls in range(CLASSES):
        value = jnp.sum(wide * row(CW + cls), -1, keepdims=True)
        value = value + class_bias_ref[layer, cls]
        logits = jnp.where(lanes == cls, value, logits)
    logits_ref[...] = logits[0:8]
    valid = lanes < CLASSES
    peak = jnp.max(jnp.where(valid, logits, -jnp.inf), -1, keepdims=True)
    shifted = jnp.where(valid, jnp.exp(logits - peak), 0.0)
    soft = shifted / jnp.sum(shifted, -1, keepdims=True)
    label = jnp.where(rows == 0, labels_ref[0], labels_ref[1])
    logit_grad = (soft - (lanes == label).astype(F32)).astype(BF16)
    logit_wide = logit_grad.astype(F32)
    back = jnp.zeros((16, D), F32)
    for cls in range(CLASSES):
        picked = jnp.sum(jnp.where(lanes == cls, logit_wide, 0.0), -1, keepdims=True)
        back = back + picked * row(CW + cls)
    pool_grad = (back * (1.0 - pooled * pooled)).astype(BF16)
    first_grad_ref[...] = nt(pool_grad, pool_weight)[0:8]
    padded = jnp.concatenate([logit_wide[0:2], jnp.zeros((2, D - 128), F32)], -1)
    ramp_ref[...] = jnp.concatenate(
        [first.astype(F32)[0:2], pool_grad.astype(F32)[0:2], wide[0:2], padded], 0
    ).astype(BF16)


def ffn_forward(layer, labels, class_bias, normed, low, small, in_bias, weights):
    tokens = low.shape[0]
    shapes = (
        ((2, tokens, D), BF16),
        ((2, tokens, D), BF16),
        ((4, tokens, D), F32),
        ((tokens, D), F32),
        ((tokens, 1), F32),
        ((tokens, D), BF16),
        ((8, 128), F32),
        ((8, D), BF16),
        ((8, D), F32),
    )
    smem = pl.BlockSpec(memory_space=pltpu.SMEM)
    return pl.pallas_call(
        functools.partial(ffn_forward_kernel, layer),
        out_shape=tuple(jax.ShapeDtypeStruct(*item) for item in shapes),
        in_specs=[smem, smem] + [vmem()] * 4 + [anywhere()] * 10,
        out_specs=tuple(vmem() for _ in shapes),
        scratch_shapes=[
            pltpu.VMEM((4, D, D), BF16),
            pltpu.VMEM((SHARDS, 4, PART, D), BF16),
            pltpu.VMEM((SHARDS, 4, POOL_PART, D), BF16),
            pltpu.VMEM((4, tokens, D), BF16),
            pltpu.SemaphoreType.DMA((30,)),
        ],
        compiler_params=pltpu.CompilerParams(vmem_limit_bytes=VMEM_LIMIT),
        cost_estimate=cost(11),
        name="ffn_forward%d" % layer,
    )(labels, class_bias, normed, low, small, in_bias, *weights)


def ffn_backward_kernel(
    layer, grad_ref, first_ref, normed_two_ref, rstd_two_ref, slope_ref, normed_ref, rstd_ref, small,
    *refs
):
    weights = refs[:10]
    pairs_ref, rows_ref, low_ref, smalls_ref = refs[10:14]
    up, down, sems = refs[14:]
    copies = load_ffn_weights(weights, up, down, None, sems)

    def row(index):
        return small[layer, index : index + 1].astype(F32)

    grad = grad_ref[...].astype(F32)
    index = lax.broadcasted_iota(jnp.int32, grad.shape, 0)
    grad = grad + jnp.where(index == 0, first_ref[0:1], 0.0)
    grad = grad + jnp.where(index == SEQ, first_ref[1:2], 0.0)
    res_two, gain_two, shift_two = norm_back(grad, normed_two_ref[...], rstd_two_ref[...], row(G1))
    ffn_grad = res_two.astype(BF16)
    pairs_ref[4] = ffn_grad
    for item in copies:
        item.wait()
    middle_grad = res_two
    for block in range(4):
        act_grad = nt(ffn_grad, down[block].reshape(D, D))
        pre_grad = (act_grad * slope_ref[block]).astype(BF16)
        pairs_ref[block] = pre_grad
        smalls_ref[block : block + 1] = jnp.sum(pre_grad.astype(F32), 0, keepdims=True)
        middle_grad = middle_grad + nt(pre_grad, up[block])
    res_one, gain_one, shift_one = norm_back(middle_grad, normed_ref[...], rstd_ref[...], row(G0))
    rows_ref[...] = res_one
    low = res_one.astype(BF16)
    low_ref[...] = low
    smalls_ref[4:5] = jnp.sum(ffn_grad.astype(F32), 0, keepdims=True)
    smalls_ref[5:6] = jnp.sum(low.astype(F32), 0, keepdims=True)
    smalls_ref[6:7] = gain_one
    smalls_ref[7:8] = gain_two
    smalls_ref[8:9] = shift_one
    smalls_ref[9:10] = shift_two


def ffn_backward(
    layer, grad, first_grad, normed_two, rstd_two, slope, normed, rstd, small, weights
):
    tokens = grad.shape[0]
    shapes = (
        ((5, tokens, D), BF16),
        ((tokens, D), F32),
        ((tokens, D), BF16),
        ((10, D), F32),
    )
    return pl.pallas_call(
        functools.partial(ffn_backward_kernel, layer),
        out_shape=tuple(jax.ShapeDtypeStruct(*item) for item in shapes),
        in_specs=[vmem()] * 8 + [anywhere()] * 10,
        out_specs=tuple(vmem() for _ in shapes),
        scratch_shapes=[
            pltpu.VMEM((4, D, D), BF16),
            pltpu.VMEM((SHARDS, 4, PART, D), BF16),
            pltpu.SemaphoreType.DMA((20,)),
        ],
        compiler_params=pltpu.CompilerParams(vmem_limit_bytes=VMEM_LIMIT),
        cost_estimate=cost(9),
        name="ffn_backward%d" % layer,
    )(grad, first_grad, normed_two, rstd_two, slope, normed, rstd, small, *weights)


def ffn_weights_kernel(
    act_ref, act_near_ref, parts_ref, parts_near_ref, pairs_ref, pairs_near_ref, keep_ref, send_ref
):
    place = piece_index()
    for slot in range(2):
        target = send_ref if slot else keep_ref
        down_grad = tn(act_ref[slot], pairs_ref[4]) + tn(act_near_ref[slot], pairs_near_ref[4])
        down_grad = down_grad.astype(BF16)
        for block in range(4):
            target[(4 + block) ^ place] = down_grad[block * PART : (block + 1) * PART]
            up_grad = tn(parts_ref[slot], pairs_ref[block])
            up_grad = up_grad + tn(parts_near_ref[slot], pairs_near_ref[block])
            target[block ^ place] = up_grad.astype(BF16)


def ffn_weight_grads(layer, act, act_near, parts, parts_near, pairs, pairs_near):
    shape = jax.ShapeDtypeStruct((PIECES, PART, D), BF16)
    return pl.pallas_call(
        ffn_weights_kernel,
        out_shape=(shape, shape),
        compiler_params=pltpu.CompilerParams(vmem_limit_bytes=VMEM_LIMIT),
        cost_estimate=cost(8),
        name="ffn_weight_grads%d" % layer,
    )(act, act_near, parts, parts_near, pairs, pairs_near)


def attn_backward_kernel(res_ref, grad_ref, qkv_ref, probs_ref, *refs):
    weights = refs[:10]
    pairs_ref, pairs_send_ref, rows_ref, biases_ref = refs[10:14]
    slots, sems = refs[14:]
    copies = load_attn_weights(weights, slots, sems)
    shard = shard_index()
    grad = grad_ref[...]
    total = res_ref[...]
    for slot in range(4):
        for item in copies[slot]:
            item.wait()
        target = pairs_send_ref if slot & 1 else pairs_ref
        context_grad = nt(grad, slots[slot, 3]).astype(BF16)
        seq_rows = [[], [], []]
        for seq in range(2):
            rows = slice(seq * SEQ, (seq + 1) * SEQ)
            heads = [[], [], []]
            for head in range(PART // HEAD_DIM):
                cols = slice(head * HEAD_DIM, (head + 1) * HEAD_DIM)
                query = qkv_ref[slot, 0, rows, cols]
                key = qkv_ref[slot, 1, rows, cols]
                val = qkv_ref[slot, 2, rows, cols]
                probs = probs_ref[slot, seq * 3 + head]
                back = context_grad[rows, cols]
                prob_grad = nt(back, val)
                mean = jnp.sum(prob_grad * probs, -1, keepdims=True)
                score_grad = (probs * (prob_grad - mean)).astype(BF16)
                heads[0].append(nn(score_grad, key) * HEAD_DIM ** (-0.5))
                heads[1].append(tn(score_grad, query) * HEAD_DIM ** (-0.5))
                heads[2].append(tn(probs.astype(BF16), back))
            for part in range(3):
                seq_rows[part].append(jnp.concatenate(heads[part], -1))
        bias_rows = []
        for part in range(3):
            value = jnp.concatenate(seq_rows[part], 0).astype(BF16)
            target[slot >> 1, part] = value
            if part != 1:
                bias_rows.append(jnp.sum(value.astype(F32), 0, keepdims=True))
            total = total + nn(value, slots[slot, part])
        biases_ref[shard ^ slot] = jnp.concatenate(bias_rows, 0)
    rows_ref[...] = total.astype(rows_ref.dtype)


def attn_backward(layer, res, grad, qkv, probs, weights):
    tokens = grad.shape[0]
    shapes = (
        ((2, 3, tokens, PART), BF16),
        ((2, 3, tokens, PART), BF16),
        ((tokens, D), BF16 if layer == 0 else F32),
        ((SHARDS, 2, PART), F32),
    )
    return pl.pallas_call(
        attn_backward_kernel,
        out_shape=tuple(jax.ShapeDtypeStruct(*item) for item in shapes),
        in_specs=[vmem()] * 4 + [anywhere()] * 10,
        out_specs=tuple(vmem() for _ in shapes),
        scratch_shapes=[pltpu.VMEM((4, 4, PART, D), BF16), pltpu.SemaphoreType.DMA((10,))],
        compiler_params=pltpu.CompilerParams(vmem_limit_bytes=VMEM_LIMIT),
        cost_estimate=cost(12),
        name="attn_backward%d" % layer,
    )(res, grad, qkv, probs, *weights)


def attn_weights_kernel(
    x_ref, x_near_ref, grad_ref, grad_near_ref, context_ref, context_near_ref, pairs_ref,
    pairs_near_ref, keep_ref, send_ref
):
    place = piece_index()
    half = PART // 2
    for slot in range(2):
        target = send_ref if slot else keep_ref
        for unit in range(4):
            if unit == 3:
                value = tn(context_ref[slot], grad_ref[...])
                value = value + tn(context_near_ref[slot], grad_near_ref[...])
            else:
                value = tn(pairs_ref[slot, unit], x_ref[...])
                value = value + tn(pairs_near_ref[slot, unit], x_near_ref[...])
            value = value.astype(BF16)
            for part in range(2):
                target[(2 * unit + part) ^ place] = value[part * half : (part + 1) * half]


def attn_weight_grads(layer, *operands):
    shape = jax.ShapeDtypeStruct((PIECES, PART // 2, D), BF16)
    return pl.pallas_call(
        attn_weights_kernel,
        out_shape=(shape, shape),
        compiler_params=pltpu.CompilerParams(vmem_limit_bytes=VMEM_LIMIT),
        cost_estimate=cost(6),
        name="attn_weight_grads%d" % layer,
    )(*operands)


def reduce_pieces(moves, mine, theirs):
    came = moves.row(theirs)
    dp = moves.mesh.shape["dp"]
    count = PIECES
    for bit in (1, 2, 4):
        count //= 2
        low, high = mine[:count] + came[:count], mine[count:] + came[count:]
        mine, came = low, moves.place(high, bit)
    mine = mine + came
    bit = 8
    while bit < dp:
        mine = mine + moves.place(mine, bit)
        bit *= 2
    mine = jnp.concatenate([mine, moves.place(mine, 4)], 0)
    mine = jnp.concatenate([mine, moves.place(mine, 2)], 0)
    return mine, moves.place(mine, 1)


def stacked_call(kernel, layer, pieces, shapes, previous, scratch, name):
    prior = () if previous is None else tuple(previous)
    return pl.pallas_call(
        kernel,
        out_shape=tuple(jax.ShapeDtypeStruct(shape, F32) for shape in shapes),
        in_specs=[vmem()] * 2 + [anywhere()] * len(prior),
        out_specs=tuple(anywhere() for _ in shapes),
        input_output_aliases={2 + index: index for index in range(len(prior))},
        scratch_shapes=scratch,
        compiler_params=pltpu.CompilerParams(vmem_limit_bytes=VMEM_LIMIT),
        cost_estimate=cost(3),
        name=name,
    )(*pieces, *prior)


def natural_order(near_ref, far_ref, whole):
    place = piece_index()
    for index in range(4):
        whole[index ^ place] = near_ref[index].astype(F32)
        whole[(4 + index) ^ place] = far_ref[index].astype(F32)


def ffn_unpack_kernel(layer, near_ref, far_ref, *refs):
    in_ref, down_ref, whole, sems = refs[-4:]
    natural_order(near_ref, far_ref, whole)
    copies = []
    for block in range(4):
        copies.append((whole.at[block], in_ref.at[layer, :, block * D : (block + 1) * D]))
        copies.append(
            (whole.at[4 + block], down_ref.at[layer, block * PART : (block + 1) * PART])
        )
    copies = [
        pltpu.make_async_copy(src, dst, sems.at[index]) for index, (src, dst) in enumerate(copies)
    ]
    for item in copies:
        item.start()
    for item in copies:
        item.wait()


def ffn_unpack(layer, pieces, previous):
    return stacked_call(
        functools.partial(ffn_unpack_kernel, layer),
        layer,
        pieces,
        ((LAYERS, PART, FF), (LAYERS, D, D)),
        previous,
        [pltpu.VMEM((PIECES, PART, D), F32), pltpu.SemaphoreType.DMA((8,))],
        "ffn_unpack%d" % layer,
    )


def attn_unpack_kernel(layer, near_ref, far_ref, *refs):
    qkv_ref, out_ref, whole, turned, sems = refs[-5:]
    natural_order(near_ref, far_ref, whole)
    half = PART // 2
    copies = [
        pltpu.make_async_copy(
            whole.at[6 + part], out_ref.at[layer, part * half : (part + 1) * half], sems.at[part]
        )
        for part in range(2)
    ]
    for item in copies:
        item.start()
    for unit in range(3):
        turned[unit] = whole[2 * unit : 2 * unit + 2].reshape(PART, D).T
        copies.append(
            pltpu.make_async_copy(turned.at[unit], qkv_ref.at[layer, unit], sems.at[2 + unit])
        )
        copies[-1].start()
    for item in copies:
        item.wait()


def attn_unpack(layer, pieces, previous):
    return stacked_call(
        functools.partial(attn_unpack_kernel, layer),
        layer,
        pieces,
        ((LAYERS, 3, D, PART), (LAYERS, PART, D)),
        previous,
        [
            pltpu.VMEM((PIECES, PART // 2, D), F32),
            pltpu.VMEM((3, D, PART), F32),
            pltpu.SemaphoreType.DMA((5,)),
        ],
        "attn_unpack%d" % layer,
    )


def on_device(
    mesh,
    hidden_in,
    out_cotangent,
    labels,
    qkv_weight,
    qkv_bias,
    out_weight,
    out_bias,
    norm_gain,
    norm_shift,
    ffn_in,
    ffn_in_bias,
    ffn_out,
    ffn_out_bias,
    pool_weight,
    pool_bias,
    class_weight,
    class_bias,
):
    moves = Moves(mesh)
    shard = shard_index()
    packed = jnp.concatenate(
        [
            qkv_bias,
            out_bias[:, None],
            norm_gain,
            norm_shift,
            ffn_in_bias.reshape(LAYERS, 4, PART),
            ffn_out_bias[:, None],
            pool_bias[:, None],
            jnp.swapaxes(class_weight, 1, 2),
        ],
        1,
    )
    shard_small = lax.all_gather(packed, "head", axis=0)
    small = jnp.transpose(shard_small, (1, 2, 0, 3)).reshape(LAYERS, 16, D)
    in_bias = jnp.transpose(shard_small[:, :, 7:11], (1, 0, 2, 3)).reshape(LAYERS, SHARDS, D)
    class_bias_wide = class_bias.astype(F32)

    attn_weights, ffn_weights = [], []
    for layer in range(LAYERS):
        attn_weights.append(
            gather_weights(moves, *pack_attn(layer, qkv_weight, out_weight), 2)
        )
        ffn_weights.append(
            gather_weights(moves, *pack_ffn(layer, ffn_in, ffn_out, pool_weight), 1)
        )

    x = hidden_in
    kept, outputs, logits, ramps = [], [], [], []
    for layer in range(LAYERS):
        x_near = moves.core(x)
        qkv, probs, context, context_send, normed, rstd, low, parts, parts_send = attn_forward(
            layer, x, shard_small, small, attn_weights[layer]
        )
        context_near, parts_near = moves.core(context_send), moves.core(parts_send)
        act, act_send, slope, normed_two, rstd_two, output, logit, ramp, first_grad = ffn_forward(
            layer, labels, class_bias_wide, normed, low, small, in_bias, ffn_weights[layer]
        )
        act_near = moves.core(act_send)
        kept.append(
            (
                (x, x_near),
                (qkv, probs, (context, context_near), normed, rstd, (parts, parts_near)),
                ((act, act_near), slope, normed_two, rstd_two, first_grad),
            )
        )
        outputs.append(output)
        logits.append(logit[0:2, 0:CLASSES])
        ramps.append(ramp)
        x = output

    grad = out_cotangent
    attn_parts, ffn_parts, smalls = [None] * LAYERS, [None] * LAYERS, [None] * LAYERS
    for layer in reversed(range(LAYERS)):
        xs, attn_kept, ffn_kept = kept[layer]
        qkv, probs, contexts, normed, rstd, parts = attn_kept
        acts, slope, normed_two, rstd_two, first_grad = ffn_kept
        pairs, res_one, low, rows = ffn_backward(
            layer, grad, first_grad, normed_two, rstd_two, slope, normed, rstd, small,
            ffn_weights[layer],
        )
        pairs_near, low_near = moves.core(pairs), moves.core(low)
        attn_pairs, attn_pairs_send, grad, biases = attn_backward(
            layer, res_one, low, qkv, probs, attn_weights[layer]
        )
        attn_pairs_near = moves.core(attn_pairs_send)
        ffn_parts[layer] = reduce_pieces(
            moves, *ffn_weight_grads(layer, *acts, *parts, pairs, pairs_near)
        )
        attn_parts[layer] = reduce_pieces(
            moves,
            *attn_weight_grads(
                layer, *xs, low, low_near, *contexts, attn_pairs, attn_pairs_near
            ),
        )
        smalls[layer] = jnp.concatenate(
            [rows, jnp.transpose(biases, (1, 0, 2)).reshape(2, D)], 0
        )

    ffn_grads, attn_grads = None, None
    for layer in reversed(range(LAYERS)):
        ffn_grads = ffn_unpack(layer, ffn_parts[layer], ffn_grads)
        attn_grads = attn_unpack(layer, attn_parts[layer], attn_grads)
    in_grad, down_grad = ffn_grads
    qkv_grad, out_grad = attn_grads

    ramp = moves.gather(jnp.stack(ramps)[None])
    ramp = ramp.reshape(ramp.shape[0], LAYERS, 4, 2, D)
    ramp = jnp.transpose(ramp, (1, 2, 0, 3, 4)).reshape(LAYERS, 4, -1, D)
    first, pool_grad, pooled, logit_grad = (ramp[:, part] for part in range(4))
    logit_grad = logit_grad[:, :, 0:CLASSES]
    own_first = lax.dynamic_slice_in_dim(first, shard * PART, PART, 2)
    own_pooled = lax.dynamic_slice_in_dim(pooled, shard * PART, PART, 2)
    pool_weight_grad = jnp.einsum("lnd,lne->lde", own_first, pool_grad, preferred_element_type=F32)
    class_weight_grad = jnp.einsum(
        "lnd,lnc->ldc", own_pooled, logit_grad, preferred_element_type=F32
    )
    class_bias_grad = jnp.sum(logit_grad.astype(F32), 1)
    own_pool = lax.dynamic_slice_in_dim(pool_grad, shard * PART, PART, 2)
    pool_bias_grad = jnp.sum(own_pool.astype(F32), 1)

    total = lax.psum(jnp.stack(smalls), AXES)
    in_bias_grad = lax.dynamic_index_in_dim(total[:, 0:4], shard, 1, keepdims=False)
    total = lax.dynamic_slice_in_dim(total[:, 4:], shard * PART, PART, 2)
    return (
        jnp.stack(outputs),
        jnp.stack(logits),
        grad,
        qkv_grad,
        total[:, 6:8],
        out_grad,
        total[:, 1],
        total[:, 2:4],
        total[:, 4:6],
        in_grad,
        in_bias_grad,
        down_grad,
        total[:, 0],
        pool_weight_grad,
        pool_bias_grad,
        class_weight_grad,
        class_bias_grad,
    )


def solution(mesh):
    return jax.shard_map(
        functools.partial(on_device, mesh),
        mesh=mesh,
        in_specs=(
            P(("dp", "head"), None),
            P(("dp", "head"), None),
            P(("dp", "head")),
            P(None, None, None, "head"),
            P(None, None, "head"),
            P(None, "head", None),
            P(None, "head"),
            P(None, None, "head"),
            P(None, None, "head"),
            P(None, "head", None),
            P(None, "head"),
            P(None, "head", None),
            P(None, "head"),
            P(None, "head", None),
            P(None, "head"),
            P(None, "head", None),
            P(),
        ),
        out_specs=(
            P(None, ("dp", "head"), None),
            P(None, ("dp", "head"), None),
            P(("dp", "head"), None),
            P(None, None, None, "head"),
            P(None, None, "head"),
            P(None, "head", None),
            P(None, "head"),
            P(None, None, "head"),
            P(None, None, "head"),
            P(None, "head", None),
            P(None, "head"),
            P(None, "head", None),
            P(None, "head"),
            P(None, "head", None),
            P(None, "head"),
            P(None, "head", None),
            P(),
        ),
        check_vma=False,
    )
```

time: 1490 us -> 718 us (0.48)
  waiting for transfers between devices: 888 us -> 380 us
  blocking collectives: 223 us -> 5.46 us
  Pallas kernels: 0 us -> 153 us
  matrix products: 122 us -> 1.7 us
  other arithmetic: 94.3 us -> 26.2 us
  local copies, waits for them, and re-layouts: 112 us -> 62.7 us
  starting transfers between devices: 25.5 us -> 67.8 us
    psum x1, waiting for transfers between devices: 442 us -> 23 us  [on_device(): total = lax.psum(jnp.stack(smalls), AXES)]
    ppermute x0 -> x83, waiting for transfers between devices: none -> 356 us  [the longest x36 236 us: place(): return lax.ppermute(value, AXES, flip(self.mesh, 'dp', bit))]
    reduce_scatter x10 -> x0, waiting for transfers between devices: 182 us -> none  [the longest x2 95.1 us: on_device(): lax.psum_scatter(parts[8].astype(jnp.bfloat16), 'head', scatter_dimension...]
    pallas_call x0 -> x20, Pallas kernels: none -> 153 us  [the longest x2 30 us: attn_backward(): pl.pallas_call(attn_backward_kernel, out_shape=tuple((jax.ShapeDtypeStruc...]
    dot_general x48 -> x2, matrix products: 122 us -> 1.7 us  [the longest x1 1.49 us: on_device(): jnp.einsum('lnd,lne->lde', own_first, pool_grad, preferred_element_type=F32)]
    unnamed x32 -> x1, waiting for transfers between devices: 107 us -> 0.02 us
    all_gather x5 -> x0, waiting for transfers between devices: 92.3 us -> none  [the longest x1 54.2 us: on_device(): lax.all_gather(ffn_out, 'head', axis=1, tiled=True)]
    psum x2 -> x0, blocking collectives: 78.3 us -> none  [the longest x1 39.6 us: on_device(): class_bias_grad = lax.psum(jnp.stack(bias_locals), ('dp', 'head'))]
  transfers between devices with their start and end apart: 30 -> 84, of which waited for: 18 -> 33; matrix products, arithmetic and copies ran while one was open for 18% -> 11% of each run, Pallas kernels for 0% -> 14%
where the time goes in v1:
time: 718 us; the launch traced here: 712 us
  waiting for transfers between devices  380 us (53%)
  Pallas kernels  153 us (21%)
  starting transfers between devices  67.8 us (9%)
  local copies, waits for them, and re-layouts  62.7 us (9%)
  other arithmetic  26.2 us (4%)
  between operations  15.3 us (2%)
    ppermute x36, waiting for transfers between devices, place(): return lax.ppermute(value, AXES, flip(self.mesh, 'dp', bit))  236 us
    ppermute x5, waiting for transfers between devices, gather(): came = lax.ppermute(value, AXES, flip(self.mesh, axis, bit))  85.5 us
    ppermute x36, starting transfers between devices, place(): return lax.ppermute(value, AXES, flip(self.mesh, 'dp', bit))  45.5 us
    ppermute x8, waiting for transfers between devices, row(): return lax.ppermute(value, AXES, flip(self.mesh, 'head', 2))  32.6 us
    pallas_call x2, Pallas kernels, attn_backward(): pl.pallas_call(attn_backward_kernel, out_shape=tuple((jax.ShapeDtypeStruc...  30 us
    unnamed x125, local copies, waits for them, and re-layouts  28.9 us
    pallas_call x2, Pallas kernels, attn_forward(): pl.pallas_call(functools.partial(attn_forward_kernel, layer), out_shape=t...  27.4 us
    pallas_call x2, Pallas kernels, ffn_forward(): pl.pallas_call(functools.partial(ffn_forward_kernel, layer), out_shape=tu...  23.8 us
  transfers between devices with their start and end apart: 84, of which 33 were waited for; matrix products, arithmetic and copies ran while one was open for 11% of the time, Pallas kernels for 14%

profile of v1, /device:TPU:0, one launch (start us, length us, event | category | flops | bytes accessed | tf_op | source)
XLA Modules:
  0.0 711.9 jit_solution(11261895577886030462)
XLA Ops:
  7.2 4.0 copy.85.qkv_ref
  19.8 5.3 collective-permute-done.1.refs_2_
  27.1 3.6 pack_ffn0.1
  34.5 3.6 pack_ffn1.1
  43.6 4.0 collective-permute-done.21.refs_4_
  49.7 10.0 %collective-permute-done.28.refs_2_ = bf16[432,768]{1,0:T(8,128)(2,1)} collective-permute-done((bf16[432,768]{1,0:T(8,128)(2,1)}, bf16[432,768]{1,0:T(8,128)(2,1)}, u32[]{:S(2)}, u32[]{:S(2)}) %collective-permute-start.28) | collective-permute-done | bytes 663584 | tf_op jit(solution)/shard_map/ppermute | solution.py:164
  62.9 6.4 collective-permute-done.22.refs_5_
  76.1 11.2 %collective-permute-done.11.refs_3_ = bf16[432,768]{1,0:T(8,128)(2,1)S(1)} collective-permute-done((bf16[432,768]{1,0:T(8,128)(2,1)}, bf16[432,768]{1,0:T(8,128)(2,1)S(1)}, u32[]{:S(2)}, u32[]{:S(2)}) %collective-permute-start.11) | collective-permute-done | bytes 663584 | tf_op jit(solution)/shard_map/ppermute | solution.py:167
  87.3 3.5 collective-permute-done.12.refs_4_
  93.3 8.3 %collective-permute-done.29.refs_3_ = bf16[432,768]{1,0:T(8,128)(2,1)} collective-permute-done((bf16[432,768]{1,0:T(8,128)(2,1)}, bf16[432,768]{1,0:T(8,128)(2,1)}, u32[]{:S(2)}, u32[]{:S(2)}) %collective-permute-start.29) | collective-permute-done | bytes 663584 | tf_op jit(solution)/shard_map/ppermute | solution.py:167
  101.6 5.7 collective-permute-done.30.refs_4_
  107.3 7.1 collective-permute-done.13.refs_5_
  116.1 14.2 %collective-permute-done.31.refs_5_ = bf16[432,768]{1,0:T(8,128)(2,1)} collective-permute-done((bf16[432,768]{1,0:T(8,128)(2,1)}, bf16[432,768]{1,0:T(8,128)(2,1)}, u32[]{:S(2)}, u32[]{:S(2)}) %collective-permute-start.31) | collective-permute-done | bytes 663584 | tf_op jit(solution)/shard_map/ppermute | solution.py:167
  137.4 5.5 all-gather
  144.4 13.5 %attn_forward0.1 = (bf16[4,3,256,192]{3,2,1,0:T(8,128)(2,1)}, f32[4,6,128,128]{3,2,1,0:T(8,128)}, bf16[2,256,192]{2,1,0:T(8,128)(2,1)}, bf16[2,256,192]{2,1,0:T(...) custom-call(bf16[256,768]{1,0:T(8,128)(2,1)} %x_ref.3, ...), custom_call_target="tpu_custom_call" | custom-call | bytes 45500000 | tf_op jit(solution)/shard_map/attn_forward0/pallas_call | solution.py:283
  157.9 11.8 %ffn_forward0.1 = (bf16[2,256,768]{2,1,0:T(8,128)(2,1)}, bf16[2,256,768]{2,1,0:T(8,128)(2,1)}, f32[4,256,768]{2,1,0:T(8,128)}, f32[256,768]{1,0:T(8,128)}, f32[2...) custom-call(s32[2]{0:T(128)} %labels_ref.3, ...), custom_call_target="tpu_custom_call" | custom-call | bytes 38500000 | tf_op jit(solution)/shard_map/ffn_forward0/pallas_call | solution.py:407
  169.8 13.9 %attn_forward1.1 = (bf16[4,3,256,192]{3,2,1,0:T(8,128)(2,1)}, f32[4,6,128,128]{3,2,1,0:T(8,128)}, bf16[2,256,192]{2,1,0:T(8,128)(2,1)}, bf16[2,256,192]{2,1,0:T(...) custom-call(bf16[256,768]{1,0:T(8,128)(2,1)} %get-tuple-element.99.x, ...), custom_call_target="tpu_custom_call" | custom-call | bytes 45500000 | tf_op jit(solution)/shard_map/attn_forward1/pallas_call | solution.py:283
  183.8 12.0 %ffn_forward1.1 = (bf16[2,256,768]{2,1,0:T(8,128)(2,1)}, bf16[2,256,768]{2,1,0:T(8,128)(2,1)}, f32[4,256,768]{2,1,0:T(8,128)}, f32[256,768]{1,0:T(8,128)}, f32[2...) custom-call(s32[2]{0:T(128)} %labels_ref.3, ...), custom_call_target="tpu_custom_call" | custom-call | bytes 38500000 | tf_op jit(solution)/shard_map/ffn_forward1/pallas_call | solution.py:407
  195.7 10.6 %ffn_backward1.1 = (bf16[5,256,768]{2,1,0:T(8,128)(2,1)}, f32[256,768]{1,0:T(8,128)}, bf16[256,768]{1,0:T(8,128)(2,1)}, f32[10,768]{1,0:T(8,128)}) custom-call(bf16[256,768]{1,0:T(8,128)(2,1)} %grad_ref.1, f32[8,768]{1,0:T(8,128)} %get-tuple-element.109.first_ref, f32[256,768]{1,0:T(8,128)} %get-tuple-element.110.normed_two_ref, ...), custom_call_target="tpu_custom_call" | custom-call | bytes 31500000 | tf_op jit(solution)/shard_map/ffn_backward1/pallas_call | solution.py:475
  206.4 15.1 %attn_backward1.1 = (bf16[2,3,256,192]{3,2,1,0:T(8,128)(2,1)}, bf16[2,3,256,192]{3,2,1,0:T(8,128)(2,1)}, f32[256,768]{1,0:T(8,128)}, f32[4,2,192]{2,1,0:T(2,128)}) custom-call(f32[256,768]{1,0:T(8,128)} %get-tuple-element.114.res_ref, bf16[256,768]{1,0:T(8,128)(2,1)} %get-tuple-element.115.grad_ref, bf16[4,3,256,192]{3,2,1,0:T(8,128)(2,1)} %get-tuple-element.116.qkv_ref, ...), custom_call_target="tpu_custom_call" | custom-call | bytes 42000000 | tf_op jit(solution)/shard_map/attn_backward1/pallas_call | solution.py:568
  221.5 10.8 %ffn_backward0.1 = (bf16[5,256,768]{2,1,0:T(8,128)(2,1)}, f32[256,768]{1,0:T(8,128)}, bf16[256,768]{1,0:T(8,128)(2,1)}, f32[10,768]{1,0:T(8,128)}) custom-call(f32[256,768]{1,0:T(8,128)} %get-tuple-element.118.grad_ref, f32[8,768]{1,0:T(8,128)} %get-tuple-element.119.first_ref, f32[256,768]{1,0:T(8,128)} %get-tuple-element.120.normed_two_ref, ...), custom_call_target="tpu_custom_call" | custom-call | bytes 31500000 | tf_op jit(solution)/shard_map/ffn_backward0/pallas_call | solution.py:475
  234.1 14.9 %attn_backward0.1 = (bf16[2,3,256,192]{3,2,1,0:T(8,128)(2,1)}, bf16[2,3,256,192]{3,2,1,0:T(8,128)(2,1)}, bf16[256,768]{1,0:T(8,128)(2,1)}, f32[4,2,192]{2,1,0:T(2,128)}) custom-call(f32[256,768]{1,0:T(8,128)} %get-tuple-element.124.res_ref, bf16[256,768]{1,0:T(8,128)(2,1)} %get-tuple-element.125.grad_ref, ...), custom_call_target="tpu_custom_call" | custom-call | bytes 42000000 | tf_op jit(solution)/shard_map/attn_backward0/pallas_call | solution.py:568
  258.5 7.3 %ffn_weight_grads0.1 = (bf16[8,192,768]{2,1,0:T(8,128)(2,1)}, bf16[8,192,768]{2,1,0:T(8,128)(2,1)}) custom-call(bf16[2,256,768]{2,1,0:T(8,128)(2,1)} %get-tuple-element.149.act_ref, bf16[2,256,768]{2,1,0:T(8,128)(2,1)} %copy-done.41, bf16[2,256,192]{2,1,0:T(8,128)(2,1)} %get-tuple-element.151.parts_ref, ...), custom_call_target="tpu_custom_call" | custom-call | bytes 28000000 | tf_op jit(solution)/shard_map/ffn_weight_grads0/pallas_call | solution.py:508
  269.2 7.1 ffn_weight_grads1.1
  289.1 82.7 %collective-permute-done.79 = bf16[2,2,8,768]{3,2,1,0:T(8,128)(2,1)} collective-permute-done((bf16[2,2,8,768]{3,2,1,0:T(8,128)(2,1)}, bf16[2,2,8,768]{3,2,1,0:T(8,128)(2,1)}, u32[]{:S(2)}, u32[]{:S(2)}) %collective-permute-start.79) | collective-permute-done | bytes 49184 | tf_op jit(solution)/shard_map/ppermute | solution.py:174
  382.4 23.0 %all-reduce.2.cloned.1.call-done = f32[2,12,768]{2,1,0:T(8,128)} async-done(((f32[2,12,768]{2,1,0:T(8,128)}), f32[2,12,768]{2,1,0:T(8,128)}) %all-reduce.2.cloned.1.call-update) | async-done | bytes 73744 | tf_op jit(solution)/shard_map/psum | solution.py:842
  416.8 4.5 attn_weight_grads0.1
  428.0 3.2 collective-permute-start.82
  431.2 4.6 attn_weight_grads1.1
  458.4 16.4 %collective-permute-done.51 = bf16[8,96,768]{2,1,0:T(8,128)(2,1)} collective-permute-done((bf16[8,96,768]{2,1,0:T(8,128)(2,1)}, bf16[8,96,768]{2,1,0:T(8,128)(2,1)}, u32[]{:S(2)}, u32[]{:S(2)}) %collective-permute-start.51) | collective-permute-done | bytes 1179680 | tf_op jit(solution)/shard_map/ppermute | solution.py:164
  479.2 3.3 collective-permute-start.63
  482.5 12.8 %collective-permute-done.72 = bf16[4,192,768]{2,1,0:T(8,128)(2,1)} collective-permute-done((bf16[4,192,768]{2,1,0:T(8,128)(2,1)}, bf16[4,192,768]{2,1,0:T(8,128)(2,1)}, u32[]{:S(2)}, u32[]{:S(2)}) %collective-permute-start.72) | collective-permute-done | bytes 1179680 | tf_op jit(solution)/shard_map/ppermute | solution.py:167
  498.2 9.7 %collective-permute-done.41 = bf16[4,96,768]{2,1,0:T(8,128)(2,1)S(1)} collective-permute-done((bf16[4,96,768]{2,1,0:T(8,128)(2,1)S(1)}, bf16[4,96,768]{2,1,0:T(8,128)(2,1)S(1)}, u32[]{:S(2)}, u32[]{:S(2)}) %collective-permute-start.41) | collective-permute-done | bytes 589856 | tf_op jit(solution)/shard_map/ppermute | solution.py:167
  509.4 9.3 %collective-permute-done.52 = bf16[4,96,768]{2,1,0:T(8,128)(2,1)S(1)} collective-permute-done((bf16[4,96,768]{2,1,0:T(8,128)(2,1)S(1)}, bf16[4,96,768]{2,1,0:T(8,128)(2,1)S(1)}, u32[]{:S(2)}, u32[]{:S(2)}) %collective-permute-start.52) | collective-permute-done | bytes 589856 | tf_op jit(solution)/shard_map/ppermute | solution.py:167
  525.0 24.9 %collective-permute-done.64 = bf16[1,192,768]{2,1,0:T(8,128)(2,1)S(1)} collective-permute-done((bf16[1,192,768]{2,1,0:T(8,128)(2,1)S(1)}, bf16[1,192,768]{2,1,0:T(8,128)(2,1)S(1)}, u32[]{:S(2)}, u32[]{:S(2)}) %collective-permute-start.64) | collective-permute-done | bytes 294944 | tf_op jit(solution)/shard_map/ppermute | solution.py:167
  550.0 14.1 %collective-permute-done.74 = bf16[1,192,768]{2,1,0:T(8,128)(2,1)S(1)} collective-permute-done((bf16[1,192,768]{2,1,0:T(8,128)(2,1)S(1)}, bf16[1,192,768]{2,1,0:T(8,128)(2,1)S(1)}, u32[]{:S(2)}, u32[]{:S(2)}) %collective-permute-start.74) | collective-permute-done | bytes 294944 | tf_op jit(solution)/shard_map/ppermute | solution.py:167
  567.2 11.2 %collective-permute-done.65 = bf16[1,192,768]{2,1,0:T(8,128)(2,1)S(1)} collective-permute-done((bf16[1,192,768]{2,1,0:T(8,128)(2,1)S(1)}, bf16[1,192,768]{2,1,0:T(8,128)(2,1)S(1)}, u32[]{:S(2)}, u32[]{:S(2)}) %collective-permute-start.65) | collective-permute-done | bytes 294944 | tf_op jit(solution)/shard_map/ppermute | solution.py:167
  578.6 5.4 collective-permute-done.75
  587.3 19.6 %collective-permute-done.44 = bf16[1,96,768]{2,1,0:T(8,128)(2,1)S(1)} collective-permute-done((bf16[1,96,768]{2,1,0:T(8,128)(2,1)S(1)}, bf16[1,96,768]{2,1,0:T(8,128)(2,1)S(1)}, u32[]{:S(2)}, u32[]{:S(2)}) %collective-permute-start.44) | collective-permute-done | bytes 147488 | tf_op jit(solution)/shard_map/ppermute | solution.py:167
  610.5 6.3 collective-permute-done.76
  618.7 4.5 collective-permute-done.45
  624.8 4.6 collective-permute-done.56
  634.6 48.2 %collective-permute-done.57.far_ref = bf16[4,96,768]{2,1,0:T(8,128)(2,1)S(1)} collective-permute-done((bf16[4,96,768]{2,1,0:T(8,128)(2,1)S(1)}, bf16[4,96,768]{2,1,0:T(8,128)(2,1)S(1)}, u32[]{:S(2)}, u32[]{:S(2)}) %collective-permute-start.57) | collective-permute-done | bytes 589856 | tf_op jit(solution)/shard_map/ppermute | solution.py:167
  683.6 3.1 attn_unpack1.1
  687.5 3.1 attn_unpack0.1
  690.6 5.6 copy.96
  696.3 4.2 ffn_unpack1.1
  700.5 4.2 ffn_unpack0.1
  (344 shorter events, 159.1 us)
Async XLA Ops:
  7.2 398.3 %all-reduce.2.cloned.1.call-start = ((), (), s32[]{:S(2)}) async-start(), calls=%async_computation | async-start | bytes 196608 | tf_op jit(solution)/shard_map/psum | solution.py:842
  38.0 21.6 %collective-permute-start.28 = (bf16[432,768]{1,0:T(8,128)(2,1)}, bf16[432,768]{1,0:T(8,128)(2,1)}, u32[]{:S(2)}, u32[]{:S(2)}) collective-permute-start(bf16[432,768]{1,0:T(8,128)(2,1)} %get-tuple-element.105), channel_id=1, source_target_pairs={{0,2},{1,3},{2,0},{3,1},{4,6},{5,7},{6,4},{7,5},{8,10},{9,11},{10,... | collective-permute-start | bytes 1990664 | tf_op jit(solution)/shard_map/ppermute | solution.py:164
  43.6 28.6 %collective-permute-start = (bf16[4,192,768]{2,1,0:T(8,128)(2,1)S(1)}, bf16[4,192,768]{2,1,0:T(8,128)(2,1)S(1)}, u32[]{:S(2)}, u32[]{:S(2)}) collective-permute-start(bf16[4,192,768]{2,1,0:T(8,128)(2,1)S(1)} %copy-done.2), channel_id=1, source_target_pairs={{0,1},{1,0},{2,3},{3,2},{4,5},{5,4},{6,7},{7,6},{8,9},{9,8},{10,11... | collective-permute-start | bytes 3538952 | tf_op jit(solution)/shard_map/ppermute | solution.py:161
  49.7 25.5 %collective-permute-start.18 = (bf16[4,192,768]{2,1,0:T(8,128)(2,1)S(1)}, bf16[4,192,768]{2,1,0:T(8,128)(2,1)S(1)}, u32[]{:S(2)}, u32[]{:S(2)}) collective-permute-start(bf16[4,192,768]{2,1,0:T(8,128)(2,1)S(1)} %copy-done.4), channel_id=1, source_target_pairs={{0,1},{1,0},{2,3},{3,2},{4,5},{5,4},{6,7},{7,6},{8,9},{9,8},{10,11... | collective-permute-start | bytes 3538952 | tf_op jit(solution)/shard_map/ppermute | solution.py:161
  62.7 67.6 %collective-permute-start.9 = (bf16[4,432,768]{2,1,0:T(8,128)(2,1)S(1)}, bf16[4,432,768]{2,1,0:T(8,128)(2,1)S(1)}, u32[]{:S(2)}, u32[]{:S(2)}) collective-permute-start(bf16[4,432,768]{2,1,0:T(8,128)(2,1)S(1)} %copy-done), channel_id=1, source_target_pairs={{0,1},{1,0},{2,3},{3,2},{4,5},{5,4},{6,7},{7,6},{8,9},{9,8},{10,11... | collective-permute-start | bytes 7962632 | tf_op jit(solution)/shard_map/ppermute | solution.py:161
  75.2 26.4 %collective-permute-start.29 = (bf16[432,768]{1,0:T(8,128)(2,1)}, bf16[432,768]{1,0:T(8,128)(2,1)}, u32[]{:S(2)}, u32[]{:S(2)}) collective-permute-start(bf16[432,768]{1,0:T(8,128)(2,1)} %collective-permute-done.28.refs_2_), channel_id=1, source_target_pairs={{0,4},{1,5},{2,6},{3,7},{4,0},{5,1},{6,2},{7,3},{8,12},{9,13},{10,... | collective-permute-start | bytes 1990664 | tf_op jit(solution)/shard_map/ppermute | solution.py:167
  87.3 96.4 %collective-permute-start.27 = (bf16[4,432,768]{2,1,0:T(8,128)(2,1)}, bf16[4,432,768]{2,1,0:T(8,128)(2,1)}, u32[]{:S(2)}, u32[]{:S(2)}) collective-permute-start(bf16[4,432,768]{2,1,0:T(8,128)(2,1)} %get-tuple-element.104.refs_0_), channel_id=1, source_target_pairs={{0,1},{1,0},{2,3},{3,2},{4,5},{5,4},{6,7},{7,6},{8,9},{9,8},{10,11... | collective-permute-start | bytes 7962632 | tf_op jit(solution)/shard_map/ppermute | solution.py:161
  92.4 22.0 %collective-permute-start.13 = (bf16[432,768]{1,0:T(8,128)(2,1)S(1)}, bf16[432,768]{1,0:T(8,128)(2,1)S(1)}, u32[]{:S(2)}, u32[]{:S(2)}) collective-permute-start(bf16[432,768]{1,0:T(8,128)(2,1)S(1)} %collective-permute-done.12.refs_4_), channel_id=1, source_target_pairs={{0,4},{1,5},{2,6},{3,7},{4,0},{5,1},{6,2},{7,3},{8,12},{9,13},{10,... | collective-permute-start | bytes 1990664 | tf_op jit(solution)/shard_map/ppermute | solution.py:167
  115.6 68.1 %collective-permute-start.32 = (bf16[432,768]{1,0:T(8,128)(2,1)}, bf16[432,768]{1,0:T(8,128)(2,1)}, u32[]{:S(2)}, u32[]{:S(2)}) collective-permute-start(bf16[432,768]{1,0:T(8,128)(2,1)} %collective-permute-done.28.refs_2_), channel_id=1, source_target_pairs={{0,1},{1,0},{2,3},{3,2},{4,5},{5,4},{6,7},{7,6},{8,9},{9,8},{10,11... | collective-permute-start | bytes 1990664 | tf_op jit(solution)/shard_map/ppermute | solution.py:161
  130.3 53.5 %collective-permute-start.33 = (bf16[432,768]{1,0:T(8,128)(2,1)}, bf16[432,768]{1,0:T(8,128)(2,1)}, u32[]{:S(2)}, u32[]{:S(2)}) collective-permute-start(bf16[432,768]{1,0:T(8,128)(2,1)} %collective-permute-done.29.refs_3_), channel_id=1, source_target_pairs={{0,1},{1,0},{2,3},{3,2},{4,5},{5,4},{6,7},{7,6},{8,9},{9,8},{10,11... | collective-permute-start | bytes 1990664 | tf_op jit(solution)/shard_map/ppermute | solution.py:161
  131.8 51.9 %collective-permute-start.34 = (bf16[432,768]{1,0:T(8,128)(2,1)}, bf16[432,768]{1,0:T(8,128)(2,1)}, u32[]{:S(2)}, u32[]{:S(2)}) collective-permute-start(bf16[432,768]{1,0:T(8,128)(2,1)} %collective-permute-done.30.refs_4_), channel_id=1, source_target_pairs={{0,1},{1,0},{2,3},{3,2},{4,5},{5,4},{6,7},{7,6},{8,9},{9,8},{10,11... | collective-permute-start | bytes 1990664 | tf_op jit(solution)/shard_map/ppermute | solution.py:161
  133.2 50.5 %collective-permute-start.35 = (bf16[432,768]{1,0:T(8,128)(2,1)}, bf16[432,768]{1,0:T(8,128)(2,1)}, u32[]{:S(2)}, u32[]{:S(2)}) collective-permute-start(bf16[432,768]{1,0:T(8,128)(2,1)} %collective-permute-done.31.refs_5_), channel_id=1, source_target_pairs={{0,1},{1,0},{2,3},{3,2},{4,5},{5,4},{6,7},{7,6},{8,9},{9,8},{10,11... | collective-permute-start | bytes 1990664 | tf_op jit(solution)/shard_map/ppermute | solution.py:161
  232.3 24.9 %collective-permute-start.60 = (bf16[5,256,768]{2,1,0:T(8,128)(2,1)}, bf16[5,256,768]{2,1,0:T(8,128)(2,1)S(1)}, u32[]{:S(2)}, u32[]{:S(2)}) collective-permute-start(bf16[5,256,768]{2,1,0:T(8,128)(2,1)} %get-tuple-element.153.pairs_ref), channel_id=1, source_target_pairs={{0,1},{1,0},{2,3},{3,2},{4,5},{5,4},{6,7},{7,6},{8,9},{9,8},{10,11... | collective-permute-start | bytes 5898248 | tf_op jit(solution)/shard_map/ppermute | solution.py:161
  232.7 36.3 %collective-permute-start.70 = (bf16[5,256,768]{2,1,0:T(8,128)(2,1)}, bf16[5,256,768]{2,1,0:T(8,128)(2,1)}, u32[]{:S(2)}, u32[]{:S(2)}) collective-permute-start(bf16[5,256,768]{2,1,0:T(8,128)(2,1)} %get-tuple-element.160.pairs_ref), channel_id=1, source_target_pairs={{0,1},{1,0},{2,3},{3,2},{4,5},{5,4},{6,7},{7,6},{8,9},{9,8},{10,11... | collective-permute-start | bytes 5898248 | tf_op jit(solution)/shard_map/ppermute | solution.py:161
  232.9 23.9 %collective-permute-start.58 = (bf16[2,256,768]{2,1,0:T(8,128)(2,1)}, bf16[2,256,768]{2,1,0:T(8,128)(2,1)S(1)}, u32[]{:S(2)}, u32[]{:S(2)}) collective-permute-start(bf16[2,256,768]{2,1,0:T(8,128)(2,1)} %get-tuple-element.150), channel_id=1, source_target_pairs={{0,1},{1,0},{2,3},{3,2},{4,5},{5,4},{6,7},{7,6},{8,9},{9,8},{10,11... | collective-permute-start | bytes 2359304 | tf_op jit(solution)/shard_map/ppermute | solution.py:161
  233.2 23.4 %collective-permute-start.59 = (bf16[2,256,192]{2,1,0:T(8,128)(2,1)}, bf16[2,256,192]{2,1,0:T(8,128)(2,1)}, u32[]{:S(2)}, u32[]{:S(2)}) collective-permute-start(bf16[2,256,192]{2,1,0:T(8,128)(2,1)} %get-tuple-element.152), channel_id=1, source_target_pairs={{0,1},{1,0},{2,3},{3,2},{4,5},{5,4},{6,7},{7,6},{8,9},{9,8},{10,11... | collective-permute-start | bytes 589832 | tf_op jit(solution)/shard_map/ppermute | solution.py:161
  256.6 122.8 %collective-permute-start.36 = (bf16[256,768]{1,0:T(8,128)(2,1)}, bf16[256,768]{1,0:T(8,128)(2,1)}, u32[]{:S(2)}, u32[]{:S(2)}) collective-permute-start(bf16[256,768]{1,0:T(8,128)(2,1)} %x_ref.3), channel_id=1, source_target_pairs={{0,1},{1,0},{2,3},{3,2},{4,5},{5,4},{6,7},{7,6},{8,9},{9,8},{10,11... | collective-permute-start | bytes 1179656 | tf_op jit(solution)/shard_map/ppermute | solution.py:161
  265.7 170.7 %collective-permute-start.61 = (bf16[8,192,768]{2,1,0:T(8,128)(2,1)}, bf16[8,192,768]{2,1,0:T(8,128)(2,1)S(1)}, u32[]{:S(2)}, u32[]{:S(2)}) collective-permute-start(bf16[8,192,768]{2,1,0:T(8,128)(2,1)} %get-tuple-element.155), channel_id=1, source_target_pairs={{0,2},{1,3},{2,0},{3,1},{4,6},{5,7},{6,4},{7,5},{8,10},{9,11},{10,... | collective-permute-start | bytes 7077896 | tf_op jit(solution)/shard_map/ppermute | solution.py:164
  268.5 110.9 %collective-permute-start.38 = (bf16[2,256,192]{2,1,0:T(8,128)(2,1)}, bf16[2,256,192]{2,1,0:T(8,128)(2,1)}, u32[]{:S(2)}, u32[]{:S(2)}) collective-permute-start(bf16[2,256,192]{2,1,0:T(8,128)(2,1)} %get-tuple-element.130), channel_id=1, source_target_pairs={{0,1},{1,0},{2,3},{3,2},{4,5},{5,4},{6,7},{7,6},{8,9},{9,8},{10,11... | collective-permute-start | bytes 589832 | tf_op jit(solution)/shard_map/ppermute | solution.py:161
  276.3 165.9 %collective-permute-start.71 = (bf16[8,192,768]{2,1,0:T(8,128)(2,1)}, bf16[8,192,768]{2,1,0:T(8,128)(2,1)}, u32[]{:S(2)}, u32[]{:S(2)}) collective-permute-start(bf16[8,192,768]{2,1,0:T(8,128)(2,1)} %get-tuple-element.162), channel_id=1, source_target_pairs={{0,2},{1,3},{2,0},{3,1},{4,6},{5,7},{6,4},{7,5},{8,10},{9,11},{10,... | collective-permute-start | bytes 7077896 | tf_op jit(solution)/shard_map/ppermute | solution.py:164
  284.9 86.9 %collective-permute-start.79 = (bf16[2,2,8,768]{3,2,1,0:T(8,128)(2,1)}, bf16[2,2,8,768]{3,2,1,0:T(8,128)(2,1)}, u32[]{:S(2)}, u32[]{:S(2)}) collective-permute-start(bf16[2,2,8,768]{3,2,1,0:T(8,128)(2,1)} %pad_maximum_fusion.12), channel_id=1, source_target_pairs={{0,2},{1,3},{2,0},{3,1},{4,6},{5,7},{6,4},{7,5},{8,10},{9,11},{10,... | collective-permute-start | bytes 147464 | tf_op jit(solution)/shard_map/ppermute | solution.py:174
  377.3 34.0 %collective-permute-start.39 = (bf16[2,3,256,192]{2,3,1,0:T(8,128)(2,1)}, bf16[2,3,256,192]{2,3,1,0:T(8,128)(2,1)}, u32[]{:S(2)}, u32[]{:S(2)}) collective-permute-start(bf16[2,3,256,192]{2,3,1,0:T(8,128)(2,1)} %copy.88), channel_id=1, source_target_pairs={{0,1},{1,0},{2,3},{3,2},{4,5},{5,4},{6,7},{7,6},{8,9},{9,8},{10,11... | collective-permute-start | bytes 1769480 | tf_op jit(solution)/shard_map/ppermute | solution.py:161
  379.4 27.8 %collective-permute-start.49 = (bf16[2,256,192]{2,1,0:T(8,128)(2,1)}, bf16[2,256,192]{2,1,0:T(8,128)(2,1)}, u32[]{:S(2)}, u32[]{:S(2)}) collective-permute-start(bf16[2,256,192]{2,1,0:T(8,128)(2,1)} %get-tuple-element.136), channel_id=1, source_target_pairs={{0,1},{1,0},{2,3},{3,2},{4,5},{5,4},{6,7},{7,6},{8,9},{9,8},{10,11... | collective-permute-start | bytes 589832 | tf_op jit(solution)/shard_map/ppermute | solution.py:161
  379.5 27.8 %collective-permute-start.81 = (bf16[8,2,8,768]{3,2,1,0:T(8,128)(2,1)}, bf16[8,2,8,768]{3,2,1,0:T(8,128)(2,1)}, u32[]{:S(2)}, u32[]{:S(2)}) collective-permute-start(bf16[8,2,8,768]{3,2,1,0:T(8,128)(2,1)} %pad_maximum_fusion.9), channel_id=1, source_target_pairs={{0,8},{1,9},{2,10},{3,11},{4,12},{5,13},{6,14},{7,15},{8,0},{9,1},... | collective-permute-start | bytes 589832 | tf_op jit(solution)/shard_map/ppermute | solution.py:174
  411.3 19.9 %collective-permute-start.48 = (bf16[256,768]{1,0:T(8,128)(2,1)S(1)}, bf16[256,768]{1,0:T(8,128)(2,1)}, u32[]{:S(2)}, u32[]{:S(2)}) collective-permute-start(bf16[256,768]{1,0:T(8,128)(2,1)S(1)} %copy-done.23), channel_id=1, source_target_pairs={{0,1},{1,0},{2,3},{3,2},{4,5},{5,4},{6,7},{7,6},{8,9},{9,8},{10,11... | collective-permute-start | bytes 1179656 | tf_op jit(solution)/shard_map/ppermute | solution.py:161
  421.3 33.9 %collective-permute-start.40 = (bf16[8,96,768]{2,1,0:T(8,128)(2,1)}, bf16[8,96,768]{2,1,0:T(8,128)(2,1)}, u32[]{:S(2)}, u32[]{:S(2)}) collective-permute-start(bf16[8,96,768]{2,1,0:T(8,128)(2,1)} %get-tuple-element.134), channel_id=1, source_target_pairs={{0,2},{1,3},{2,0},{3,1},{4,6},{5,7},{6,4},{7,5},{8,10},{9,11},{10,... | collective-permute-start | bytes 3538952 | tf_op jit(solution)/shard_map/ppermute | solution.py:164
  428.0 21.0 %collective-permute-start.82 = (bf16[16,2,8,768]{3,2,1,0:T(8,128)(2,1)}, bf16[16,2,8,768]{3,2,1,0:T(8,128)(2,1)S(1)}, u32[]{:S(2)}, u32[]{:S(2)}) collective-permute-start(bf16[16,2,8,768]{3,2,1,0:T(8,128)(2,1)} %constant_dynamic-update-slice_fusion), channel_id=1, source_target_pairs={{0,16},{1,17},{2,18},{3,19},{4,20},{5,21},{6,22},{7,23},{8,24},{9,... | collective-permute-start | bytes 1179656 | tf_op jit(solution)/shard_map/ppermute | solution.py:174
  435.8 39.0 %collective-permute-start.51 = (bf16[8,96,768]{2,1,0:T(8,128)(2,1)}, bf16[8,96,768]{2,1,0:T(8,128)(2,1)}, u32[]{:S(2)}, u32[]{:S(2)}) collective-permute-start(bf16[8,96,768]{2,1,0:T(8,128)(2,1)} %get-tuple-element.140), channel_id=1, source_target_pairs={{0,2},{1,3},{2,0},{3,1},{4,6},{5,7},{6,4},{7,5},{8,10},{9,11},{10,... | collective-permute-start | bytes 3538952 | tf_op jit(solution)/shard_map/ppermute | solution.py:164
  440.8 37.0 %collective-permute-start.62 = (bf16[4,192,768]{2,1,0:T(8,128)(2,1)}, bf16[4,192,768]{2,1,0:T(8,128)(2,1)}, u32[]{:S(2)}, u32[]{:S(2)}) collective-permute-start(bf16[4,192,768]{2,1,0:T(8,128)(2,1)} %get-tuple-element.240), channel_id=1, source_target_pairs={{0,4},{1,5},{2,6},{3,7},{4,0},{5,1},{6,2},{7,3},{8,12},{9,13},{10,... | collective-permute-start | bytes 3538952 | tf_op jit(solution)/shard_map/ppermute | solution.py:167
  445.2 50.1 %collective-permute-start.72 = (bf16[4,192,768]{2,1,0:T(8,128)(2,1)}, bf16[4,192,768]{2,1,0:T(8,128)(2,1)}, u32[]{:S(2)}, u32[]{:S(2)}) collective-permute-start(bf16[4,192,768]{2,1,0:T(8,128)(2,1)} %get-tuple-element.238), channel_id=1, source_target_pairs={{0,4},{1,5},{2,6},{3,7},{4,0},{5,1},{6,2},{7,3},{8,12},{9,13},{10,... | collective-permute-start | bytes 3538952 | tf_op jit(solution)/shard_map/ppermute | solution.py:167
  457.0 50.9 %collective-permute-start.41 = (bf16[4,96,768]{2,1,0:T(8,128)(2,1)S(1)}, bf16[4,96,768]{2,1,0:T(8,128)(2,1)S(1)}, u32[]{:S(2)}, u32[]{:S(2)}) collective-permute-start(bf16[4,96,768]{2,1,0:T(8,128)(2,1)S(1)} %get-tuple-element.248), channel_id=1, source_target_pairs={{0,4},{1,5},{2,6},{3,7},{4,0},{5,1},{6,2},{7,3},{8,12},{9,13},{10,... | collective-permute-start | bytes 1769480 | tf_op jit(solution)/shard_map/ppermute | solution.py:167
  476.3 42.5 %collective-permute-start.52 = (bf16[4,96,768]{2,1,0:T(8,128)(2,1)S(1)}, bf16[4,96,768]{2,1,0:T(8,128)(2,1)S(1)}, u32[]{:S(2)}, u32[]{:S(2)}) collective-permute-start(bf16[4,96,768]{2,1,0:T(8,128)(2,1)S(1)} %get-tuple-element.246), channel_id=1, source_target_pairs={{0,4},{1,5},{2,6},{3,7},{4,0},{5,1},{6,2},{7,3},{8,12},{9,13},{10,... | collective-permute-start | bytes 1769480 | tf_op jit(solution)/shard_map/ppermute | solution.py:167
  479.2 41.1 %collective-permute-start.63 = (bf16[2,192,768]{2,1,0:T(8,128)(2,1)S(1)}, bf16[2,192,768]{2,1,0:T(8,128)(2,1)S(1)}, u32[]{:S(2)}, u32[]{:S(2)}) collective-permute-start(bf16[2,192,768]{2,1,0:T(8,128)(2,1)S(1)} %get-tuple-element.244), channel_id=1, source_target_pairs={{0,8},{1,9},{2,10},{3,11},{4,12},{5,13},{6,14},{7,15},{8,0},{9,1},... | collective-permute-start | bytes 1769480 | tf_op jit(solution)/shard_map/ppermute | solution.py:167
  496.7 25.2 %collective-permute-start.73 = (bf16[2,192,768]{2,1,0:T(8,128)(2,1)S(1)}, bf16[2,192,768]{2,1,0:T(8,128)(2,1)S(1)}, u32[]{:S(2)}, u32[]{:S(2)}) collective-permute-start(bf16[2,192,768]{2,1,0:T(8,128)(2,1)S(1)} %get-tuple-element.242), channel_id=1, source_target_pairs={{0,8},{1,9},{2,10},{3,11},{4,12},{5,13},{6,14},{7,15},{8,0},{9,1},... | collective-permute-start | bytes 1769480 | tf_op jit(solution)/shard_map/ppermute | solution.py:167
  518.8 45.4 %collective-permute-start.53 = (bf16[2,96,768]{2,1,0:T(8,128)(2,1)S(1)}, bf16[2,96,768]{2,1,0:T(8,128)(2,1)S(1)}, u32[]{:S(2)}, u32[]{:S(2)}) collective-permute-start(bf16[2,96,768]{2,1,0:T(8,128)(2,1)S(1)} %get-tuple-element.250), channel_id=1, source_target_pairs={{0,8},{1,9},{2,10},{3,11},{4,12},{5,13},{6,14},{7,15},{8,0},{9,1},... | collective-permute-start | bytes 884744 | tf_op jit(solution)/shard_map/ppermute | solution.py:167
  520.3 29.6 %collective-permute-start.64 = (bf16[1,192,768]{2,1,0:T(8,128)(2,1)S(1)}, bf16[1,192,768]{2,1,0:T(8,128)(2,1)S(1)}, u32[]{:S(2)}, u32[]{:S(2)}) collective-permute-start(bf16[1,192,768]{2,1,0:T(8,128)(2,1)S(1)} %slice_add_fusion.14), channel_id=1, source_target_pairs={{0,16},{1,17},{2,18},{3,19},{4,20},{5,21},{6,22},{7,23},{8,24},{9,... | collective-permute-start | bytes 884744 | tf_op jit(solution)/shard_map/ppermute | solution.py:167
  521.9 42.2 %collective-permute-start.74 = (bf16[1,192,768]{2,1,0:T(8,128)(2,1)S(1)}, bf16[1,192,768]{2,1,0:T(8,128)(2,1)S(1)}, u32[]{:S(2)}, u32[]{:S(2)}) collective-permute-start(bf16[1,192,768]{2,1,0:T(8,128)(2,1)S(1)} %slice_add_fusion.12), channel_id=1, source_target_pairs={{0,16},{1,17},{2,18},{3,19},{4,20},{5,21},{6,22},{7,23},{8,24},{9,... | collective-permute-start | bytes 884744 | tf_op jit(solution)/shard_map/ppermute | solution.py:167
  523.4 60.7 %collective-permute-start.43 = (bf16[1,96,768]{2,1,0:T(8,128)(2,1)S(1)}, bf16[1,96,768]{2,1,0:T(8,128)(2,1)S(1)}, u32[]{:S(2)}, u32[]{:S(2)}) collective-permute-start(bf16[1,96,768]{2,1,0:T(8,128)(2,1)S(1)} %slice_add_fusion.22), channel_id=1, source_target_pairs={{0,16},{1,17},{2,18},{3,19},{4,20},{5,21},{6,22},{7,23},{8,24},{9,... | collective-permute-start | bytes 442376 | tf_op jit(solution)/shard_map/ppermute | solution.py:167
  549.9 28.5 %collective-permute-start.65 = (bf16[1,192,768]{2,1,0:T(8,128)(2,1)S(1)}, bf16[1,192,768]{2,1,0:T(8,128)(2,1)S(1)}, u32[]{:S(2)}, u32[]{:S(2)}) collective-permute-start(bf16[1,192,768]{2,1,0:T(8,128)(2,1)S(1)} %fusion.1), channel_id=1, source_target_pairs={{0,16},{1,17},{2,18},{3,19},{4,20},{5,21},{6,22},{7,23},{8,24},{9,... | collective-permute-start | bytes 884744 | tf_op jit(solution)/shard_map/ppermute | solution.py:167
  564.3 22.9 %collective-permute-start.54 = (bf16[1,96,768]{2,1,0:T(8,128)(2,1)S(1)}, bf16[1,96,768]{2,1,0:T(8,128)(2,1)S(1)}, u32[]{:S(2)}, u32[]{:S(2)}) collective-permute-start(bf16[1,96,768]{2,1,0:T(8,128)(2,1)S(1)} %slice_add_fusion.20), channel_id=1, source_target_pairs={{0,16},{1,17},{2,18},{3,19},{4,20},{5,21},{6,22},{7,23},{8,24},{9,... | collective-permute-start | bytes 442376 | tf_op jit(solution)/shard_map/ppermute | solution.py:167
  578.5 30.4 %collective-permute-start.66 = (bf16[2,192,768]{2,1,0:T(8,128)(2,1)S(1)}, bf16[2,192,768]{2,1,0:T(8,128)(2,1)S(1)}, u32[]{:S(2)}, u32[]{:S(2)}) collective-permute-start(bf16[2,192,768]{2,1,0:T(8,128)(2,1)S(1)} %pad_maximum_fusion.5), channel_id=1, source_target_pairs={{0,8},{1,9},{2,10},{3,11},{4,12},{5,13},{6,14},{7,15},{8,0},{9,1},... | collective-permute-start | bytes 1769480 | tf_op jit(solution)/shard_map/ppermute | solution.py:167
  584.0 32.8 %collective-permute-start.76 = (bf16[2,192,768]{2,1,0:T(8,128)(2,1)S(1)}, bf16[2,192,768]{2,1,0:T(8,128)(2,1)S(1)}, u32[]{:S(2)}, u32[]{:S(2)}) collective-permute-start(bf16[2,192,768]{2,1,0:T(8,128)(2,1)S(1)} %pad_maximum_fusion.6), channel_id=1, source_target_pairs={{0,8},{1,9},{2,10},{3,11},{4,12},{5,13},{6,14},{7,15},{8,0},{9,1},... | collective-permute-start | bytes 1769480 | tf_op jit(solution)/shard_map/ppermute | solution.py:167
  584.2 22.7 %collective-permute-start.44 = (bf16[1,96,768]{2,1,0:T(8,128)(2,1)S(1)}, bf16[1,96,768]{2,1,0:T(8,128)(2,1)S(1)}, u32[]{:S(2)}, u32[]{:S(2)}) collective-permute-start(bf16[1,96,768]{2,1,0:T(8,128)(2,1)S(1)} %fusion.5), channel_id=1, source_target_pairs={{0,16},{1,17},{2,18},{3,19},{4,20},{5,21},{6,22},{7,23},{8,24},{9,... | collective-permute-start | bytes 442376 | tf_op jit(solution)/shard_map/ppermute | solution.py:167
  587.2 31.4 %collective-permute-start.55 = (bf16[1,96,768]{2,1,0:T(8,128)(2,1)S(1)}, bf16[1,96,768]{2,1,0:T(8,128)(2,1)S(1)}, u32[]{:S(2)}, u32[]{:S(2)}) collective-permute-start(bf16[1,96,768]{2,1,0:T(8,128)(2,1)S(1)} %fusion.4), channel_id=1, source_target_pairs={{0,16},{1,17},{2,18},{3,19},{4,20},{5,21},{6,22},{7,23},{8,24},{9,... | collective-permute-start | bytes 442376 | tf_op jit(solution)/shard_map/ppermute | solution.py:167
  609.0 91.5 %collective-permute-start.67 = (bf16[4,192,768]{2,1,0:T(8,128)(2,1)S(1)}, bf16[4,192,768]{2,1,0:T(8,128)(2,1)}, u32[]{:S(2)}, u32[]{:S(2)}) collective-permute-start(bf16[4,192,768]{2,1,0:T(8,128)(2,1)S(1)} %pad_maximum_fusion.near_ref), channel_id=1, source_target_pairs={{0,4},{1,5},{2,6},{3,7},{4,0},{5,1},{6,2},{7,3},{8,12},{9,13},{10,... | collective-permute-start | bytes 3538952 | tf_op jit(solution)/shard_map/ppermute | solution.py:167
  617.0 79.3 %collective-permute-start.77 = (bf16[4,192,768]{2,1,0:T(8,128)(2,1)S(1)}, bf16[4,192,768]{2,1,0:T(8,128)(2,1)}, u32[]{:S(2)}, u32[]{:S(2)}) collective-permute-start(bf16[4,192,768]{2,1,0:T(8,128)(2,1)S(1)} %pad_maximum_fusion.1.near_ref), channel_id=1, source_target_pairs={{0,4},{1,5},{2,6},{3,7},{4,0},{5,1},{6,2},{7,3},{8,12},{9,13},{10,... | collective-permute-start | bytes 3538952 | tf_op jit(solution)/shard_map/ppermute | solution.py:167
  623.3 63.4 %collective-permute-start.46 = (bf16[4,96,768]{2,1,0:T(8,128)(2,1)S(1)}, bf16[4,96,768]{2,1,0:T(8,128)(2,1)S(1)}, u32[]{:S(2)}, u32[]{:S(2)}) collective-permute-start(bf16[4,96,768]{2,1,0:T(8,128)(2,1)S(1)} %pad_maximum_fusion.3.near_ref), channel_id=1, source_target_pairs={{0,4},{1,5},{2,6},{3,7},{4,0},{5,1},{6,2},{7,3},{8,12},{9,13},{10,... | collective-permute-start | bytes 1769480 | tf_op jit(solution)/shard_map/ppermute | solution.py:167
  629.5 53.3 %collective-permute-start.57 = (bf16[4,96,768]{2,1,0:T(8,128)(2,1)S(1)}, bf16[4,96,768]{2,1,0:T(8,128)(2,1)S(1)}, u32[]{:S(2)}, u32[]{:S(2)}) collective-permute-start(bf16[4,96,768]{2,1,0:T(8,128)(2,1)S(1)} %pad_maximum_fusion.4.near_ref), channel_id=1, source_target_pairs={{0,4},{1,5},{2,6},{3,7},{4,0},{5,1},{6,2},{7,3},{8,12},{9,13},{10,... | collective-permute-start | bytes 1769480 | tf_op jit(solution)/shard_map/ppermute | solution.py:167
  (92 other events, 2024.5 us)
Sparse Core Ops, SparseCore 0:
  283.6 121.8 all-reduce.1
